TPU v7x, 512 devices: a whole 4x8x8 slice. The times are simulated.
512 devices in a mesh: queue: 32 (over y_lo, x, core), space: 16 (over y_hi, z).
Axes of the slice: x: 4, y: 8 (y_hi: 2, y_lo: 4; y = y_hi * 4 + y_lo), z: 8, core: 2. Of those that a mesh axis runs over, the one named last changes fastest.
Arguments:
- residual: bfloat16 [32, 3600, 2048], P('queue', 'space'), may hold values from -6 to 6
- head_queries: bfloat16 [32, 3600, 2048], P('queue', 'space'), may hold values from -11 to 11
- head_keys: bfloat16 [32, 3600, 2048], P('queue', 'space'), may hold values from -11 to 11
- head_values: bfloat16 [32, 3600, 2048], P('queue', 'space'), may hold values from -6 to 6
- levels: int32 [32], P('queue'), may hold values from 0 to 63, as said below
- window: int32 [32, 2], P('queue'), may hold values from 0 to 1
- level_gate: float32 [64, 2048], replicated, may hold values from 0.25 to 2
- fresh_frame: bfloat16 [3600, 2048], P('space'), may hold values from -6 to 6
Outputs:
- advanced: bfloat16 [32, 3600, 2048], P('queue', 'space')
Inputs may be any that keep to these rules, and one draw needn't show every extreme that they name: `levels`: frame f has level 2 f or 2 f + 1; the first frame has level 0 and the last 63.
All inputs are finite; a program needn't handle non-finite values.
Results may differ from a plain program's by a relative error of at most 0.004.
Values may be sent and summed in bfloat16 or wider, within the bound.
No kernel may reach another device: no remote copies, remote signals or barrier semaphores. Data moves between devices by JAX's collectives and lax.ppermute only.
A program may use at most 64 MiB of HBM per device.

v0:
```python
import math

import jax
import jax.numpy as jnp
from jax import lax
from jax.sharding import PartitionSpec as P

HEAD_DIM = 128
REACH = 1


masked_score = -1e30


def extended(shard, sides, width):
    for axis, dim in sides:
        count, length = (lax.axis_size(axis), shard.shape[dim])
        up = [(i, (i + 1) % count) for i in range(count - 1)]
        down = [(j, i) for i, j in up]
        last = lax.slice_in_dim(shard, length - width, length, axis=dim)
        leading = lax.slice_in_dim(shard, 0, width, axis=dim)
        before = lax.ppermute(last, axis, up)
        after = lax.ppermute(leading, axis, down)
        shard = jnp.concatenate([before, shard, after], axis=dim)
    return shard


def from_behind(block, axis, distance):
    devices = range(lax.axis_size(axis))
    route = [(i - distance, i) for i in devices if i - distance in devices]
    return lax.ppermute(block, axis, route)


def block_size(query_count):
    chosen = query_count
    for candidate in range(640, 7, -8):
        if query_count % candidate == 0:
            chosen = candidate
            break
    return chosen


def spatial_heads(query_part, key_part, value_part):
    scaling = 1.0 / math.sqrt(HEAD_DIM)
    query_count = query_part.shape[0]
    block_rows = block_size(query_count)
    blocks = query_part.reshape(
        query_count // block_rows, block_rows, query_part.shape[1], query_part.shape[2]
    )

    def one_block(query_block):
        scores = (
            jnp.einsum("qhd,khd->hqk", query_block, key_part, preferred_element_type=jnp.float32)
            * scaling
        )
        row_top = jnp.max(scores, axis=2, keepdims=True)
        expo_terms = jnp.exp(scores - row_top)
        row_total = jnp.sum(expo_terms, axis=2)
        weights = expo_terms.astype(jnp.bfloat16)
        summed = jnp.einsum("hqk,khd->qhd", weights, value_part, preferred_element_type=jnp.float32)
        return (summed / jnp.transpose(row_total)[:, :, None]).astype(jnp.bfloat16)

    return lax.map(one_block, blocks).reshape(query_part.shape)


def temporal_attend(
    query_part, near_keys, near_values, reach_back, reach_ahead, frame_index, frame_count
):
    scaling = 1.0 / math.sqrt(HEAD_DIM)
    window_span = near_keys.shape[0]
    reach_frames = (window_span - 1) // 2
    scores = (
        jnp.einsum("thd,jthd->jth", query_part, near_keys, preferred_element_type=jnp.float32)
        * scaling
    )
    offsets = jnp.arange(window_span, dtype=jnp.int32) - reach_frames
    target = frame_index + offsets
    usable = (
        (offsets >= -reach_back) & (offsets <= reach_ahead) & (target >= 0) & (target < frame_count)
    )
    scores = jnp.where(usable[:, None, None], scores, masked_score)
    row_top = jnp.max(scores, axis=0)
    expo_terms = jnp.exp(scores - row_top[None])
    row_total = jnp.sum(expo_terms, axis=0)
    weights = expo_terms.astype(jnp.bfloat16)
    summed = jnp.einsum("jth,jthd->thd", weights, near_values, preferred_element_type=jnp.float32)
    return summed / row_total[..., None]


def on_device(
    residual, head_queries, head_keys, head_values, levels, window, level_gate, fresh_frame
):
    tok_rows = head_queries.shape[1]
    channels = head_queries.shape[2]
    heads_total = channels // HEAD_DIM
    groups = lax.axis_size("space")
    per_group = heads_total // groups
    frame_index = lax.axis_index("queue")
    frame_count = lax.axis_size("queue")
    reach_back = window[0, 0]
    reach_ahead = window[0, 1]
    split_shape = (tok_rows, groups, per_group, HEAD_DIM)
    query_part = lax.all_to_all(
        head_queries[0].reshape(split_shape), "space", split_axis=1, concat_axis=0, tiled=True
    )
    key_part = lax.all_to_all(
        head_keys[0].reshape(split_shape), "space", split_axis=1, concat_axis=0, tiled=True
    )
    value_part = lax.all_to_all(
        head_values[0].reshape(split_shape), "space", split_axis=1, concat_axis=0, tiled=True
    )
    spatial = spatial_heads(query_part[:, 0], key_part[:, 0], value_part[:, 0])
    joined = jnp.stack([key_part[:, 0], value_part[:, 0]])[:, None]
    near_frames = extended(joined, (("queue", 1),), REACH)
    temporal = temporal_attend(
        query_part[:, 0],
        near_frames[0],
        near_frames[1],
        reach_back,
        reach_ahead,
        frame_index,
        frame_count,
    )
    spatial_wide = lax.optimization_barrier(spatial).astype(jnp.float32)
    exchanged = (spatial_wide + temporal).astype(jnp.bfloat16)[:, None]
    returned = lax.all_to_all(exchanged, "space", split_axis=0, concat_axis=1, tiled=True).reshape(
        tok_rows, channels
    )
    mixed_wide = lax.optimization_barrier(returned).astype(jnp.float32)
    chooser = (jnp.arange(level_gate.shape[0], dtype=jnp.int32) == levels[0]).astype(jnp.float32)
    gate_row = jnp.dot(chooser[None], level_gate, precision=lax.Precision.HIGHEST)[0]
    updated = (residual[0].astype(jnp.float32) + gate_row[None] * mixed_wide).astype(jnp.bfloat16)
    received = from_behind(updated[None], "queue", -1)
    is_last = frame_index == frame_count - 1
    return jnp.where(is_last, fresh_frame[None], received)


def solution(mesh):
    placed = (
        P("queue", "space", None),
        P("queue", "space", None),
        P("queue", "space", None),
        P("queue", "space", None),
        P("queue"),
        P("queue", None),
        P(),
        P("space", None),
    )
    return jax.shard_map(
        on_device, mesh=mesh, in_specs=placed, out_specs=P("queue", "space", None), check_vma=False
    )
```

profile of v0, /device:TPU:7, one launch (start us, length us, event | category | flops | bytes accessed | tf_op | source)
XLA Modules:
  0.0 261.2 jit_solution(9696843802495053473)
XLA Ops:
  2.8 15.4 %all-to-all-start.1 = ((bf16[225,16,1,128]{3,0,2,1:T(8,128)(2,1)}), bf16[225,16,1,128]{3,0,2,1:T(8,128)(2,1)S(1)}, u32[]{:S(2)}, u32[]{:S(2)}) async-start(bf16[225,16,1,128]{3,0,2,1:T(8,128)(2,1)} %copy.24), calls=%async_computation.1 | async-start | bytes 1900544 | tf_op jit(solution)/shard_map/all_to_all | solution.py:106
  19.8 20.7 %all-to-all-done.1 = bf16[225,16,1,128]{3,0,2,1:T(8,128)(2,1)S(1)} async-done(((bf16[225,16,1,128]{3,0,2,1:T(8,128)(2,1)}), bf16[225,16,1,128]{3,0,2,1:T(8,128)(2,1)S(1)}, u32[]{:S(2)}, u32[]{:S(2)}) %all-to-all-start.1) | async-done | bytes 921632 | tf_op jit(solution)/shard_map/all_to_all | solution.py:106
  40.5 11.6 %all-to-all-start.2 = ((bf16[225,16,1,128]{3,0,2,1:T(8,128)(2,1)}), bf16[225,16,1,128]{3,0,2,1:T(8,128)(2,1)S(1)}, u32[]{:S(2)}, u32[]{:S(2)}) async-start(bf16[225,16,1,128]{3,0,2,1:T(8,128)(2,1)} %copy.25), calls=%async_computation.2 | async-start | bytes 1900544 | tf_op jit(solution)/shard_map/all_to_all | solution.py:109
  53.6 21.6 %all-to-all-done.2 = bf16[225,16,1,128]{3,0,2,1:T(8,128)(2,1)S(1)} async-done(((bf16[225,16,1,128]{3,0,2,1:T(8,128)(2,1)}), bf16[225,16,1,128]{3,0,2,1:T(8,128)(2,1)S(1)}, u32[]{:S(2)}, u32[]{:S(2)}) %all-to-all-start.2) | async-done | bytes 921632 | tf_op jit(solution)/shard_map/all_to_all | solution.py:109
  75.2 10.5 %all-to-all-start = ((bf16[225,16,1,128]{3,0,2,1:T(8,128)(2,1)}), bf16[225,16,1,128]{3,0,2,1:T(8,128)(2,1)S(1)}, u32[]{:S(2)}, u32[]{:S(2)}) async-start(bf16[225,16,1,128]{3,0,2,1:T(8,128)(2,1)} %copy.23), calls=%async_computation | async-start | bytes 1900544 | tf_op jit(solution)/shard_map/all_to_all | solution.py:103
  90.0 2.9 %maximum_bitcast_fusion = bf16[2,1,3600,1,128]{4,2,0,3,1:T(8,128)(2,1)} fusion(bf16[1,3600,1,128]{3,1,2,0:T(8,128)(2,1)} %stack_squeeze.7, bf16[1,3600,1,128]{3,1,2,0:T(8,128)(2,1)} %stack_squeeze.6), kind=kLoop, calls=%fused_computation.26 | loop fusion | flops 921600 | bytes 3686400 | tf_op jit(solution)/shard_map/broadcast_in_dim | solution.py:113
  92.9 8.0 %collective-permute-start = (bf16[2,1,3600,1,128]{4,2,0,3,1:T(8,128)(2,1)}, bf16[2,1,3600,1,128]{4,2,0,3,1:T(8,128)(2,1)}, u32[]{:S(2)}, u32[]{:S(2)}) collective-permute-start(bf16[2,1,3600,1,128]{4,2,0,3,1:T(8,128)(2,1)} %maximum_bitcast_fusion), channel_id=1, source_target_pairs={{0,16},{16,32},{32,48},{48,64},{64,80},{80,96},{96,112},{112,128},... | collective-permute-start | bytes 5529608 | tf_op jit(solution)/shard_map/ppermute | solution.py:22
  103.3 2.4 squeeze.21
  105.7 2.4 all-to-all-done
  108.4 32.6 %while.10 = (s32[]{:T(128)}, bf16[6,600,1,128]{3,1,2,0:T(8,128)(2,1)}, bf16[6,600,1,128]{3,1,2,0:T(8,128)(2,1)S(1)}, bf16[3600,1,128]{2,0,1:T(8,128)(2,1)S(1)}, bf16[3600,1,128]{2,0,1:T(8,128)(2,1)}, /*index=5*/s32[]{:T(128)}) while((s32[]{:T(128)}, bf16[6,600,1,128]{3,1,2,0:T(8,128)(2,1)}, bf16[6,600,1,128]{3,1,2,0:T(8,128)(2,1)S(1)}, ...), condition=%wide.region_3.4_spmd, body=%wide.region_0.3_spmd.sunk | while | flops 1123352448 | bytes 31769412 | solution.py:63
  111.6 2.3 fusion.54
  117.0 2.3 fusion.54
  138.7 2.3 fusion.54
  143.0 3.4 %pad_maximum_fusion = bf16[2,3,3600,1,128]{4,2,0,3,1:T(8,128)(2,1)S(1)} fusion(bf16[2,1,3600,1,128]{4,2,0,3,1:T(8,128)(2,1)} %collective-permute-done.1, bf16[2,1,3600,1,128]{4,2,0,3,1:T(8,128)(2,1)} %maximum_bitcast_fusion, bf16[2,1,3600,1,128]{4,2,0,3,1:T(8,128)(2,1)} %collective-permute-done), kind=kLoop, calls=%fused_computation.17 | loop fusion | flops 5529600 | bytes 11059200 | tf_op jit(solution)/shard_map/concatenate | solution.py:24
  148.3 7.6 %fusion.28 = f32[3600,1,3]{2,1,0:T(1,128)} fusion(bf16[3600,128,1]{1,2,0:T(2,128)(2,1)} %reshape.106, bf16[3,3600,128]{2,1,0:T(8,128)(2,1)} %get-tuple-element.66), kind=kOutput, calls=%fused_computation.20 | convolution fusion | flops 2764800 | bytes 3729600 | tf_op jit(solution)/shard_map/thd,jthd->jth/dot_general | solution.py:73
  155.8 3.5 %copy.31 = f32[3600,1,3]{0,2,1:T(4,128)S(1)} copy(f32[3600,1,3]{2,1,0:T(1,128)} %fusion.28) | data formatting | bytes 86400 | tf_op jit(solution)/shard_map/thd,jthd->jth/dot_general | solution.py:73
  159.6 3.2 %copy.32 = bf16[3,3600,1]{0,2,1:T(2,128)(2,1)} copy(bf16[3,3600,1]{1,0,2:T(4,128)(2,1)S(1)} %get-tuple-element.68) | data formatting | bytes 43200 | tf_op jit(solution)/shard_map/reshape.23
  162.9 6.7 %fusion.26 = f32[3600,1,128]{2,1,0:T(1,128)} fusion(bf16[3,3600,1]{0,2,1:T(2,128)(2,1)} %copy.32, bf16[3,3600,128]{2,1,0:T(8,128)(2,1)S(1)} %get-tuple-element.65), kind=kOutput, calls=%fused_computation.18 | convolution fusion | flops 2764800 | bytes 4629600 | tf_op jit(solution)/shard_map/jth,jthd->thd/dot_general | solution.py:86
  175.2 11.9 %all-to-all-start.3 = ((bf16[16,2,14400]{2,1,0:T(2,128)(2,1)}), bf16[16,2,14400]{2,1,0:T(2,128)(2,1)S(1)}, u32[]{:S(2)}, u32[]{:S(2)}) async-start(bf16[16,2,14400]{2,1,0:T(2,128)(2,1)} %reshape.108), calls=%async_computation.3 | async-start | bytes 1851392 | tf_op jit(solution)/shard_map/all_to_all | solution.py:126
  188.1 25.6 %all-to-all-done.3 = bf16[16,2,14400]{2,1,0:T(2,128)(2,1)S(1)} async-done(((bf16[16,2,14400]{2,1,0:T(2,128)(2,1)}), bf16[16,2,14400]{2,1,0:T(2,128)(2,1)S(1)}, u32[]{:S(2)}, u32[]{:S(2)}) %all-to-all-start.3) | async-done | bytes 921632 | tf_op jit(solution)/shard_map/all_to_all | solution.py:126
  213.6 3.5 %reshape.109 = bf16[3600,1,1,128]{3,2,1,0:T(2,128)(2,1)S(1)} reshape(bf16[16,2,14400]{2,1,0:T(2,128)(2,1)S(1)} %all-to-all-done.3) | data formatting | bytes 1843200
  217.1 20.0 %reduce.8 = bf16[3600,128]{1,0:T(8,128)(2,1)} reduce(bf16[3600,1,1,128]{3,2,1,0:T(2,128)(2,1)S(1)} %reshape.109, bf16[]{:T(256)} %constant.48), dimensions={1,2}, to_apply=%all_to_all.53.reduce_sub_computation | reduce | bytes 1843202 | tf_op jit(solution)/shard_map/all_to_all | solution.py:126
  240.1 3.8 %collective-permute-start.2 = (bf16[1,225,2048]{2,1,0:T(8,128)(2,1)S(1)}, bf16[1,225,2048]{2,1,0:T(8,128)(2,1)S(1)}, u32[]{:S(2)}, u32[]{:S(2)}) collective-permute-start(bf16[1,225,2048]{2,1,0:T(8,128)(2,1)S(1)} %fusion.32), channel_id=1, source_target_pairs={{16,0},{32,16},{48,32},{64,48},{80,64},{96,80},{112,96},{128,112},... | collective-permute-start | bytes 2764808 | tf_op jit(solution)/shard_map/ppermute | solution.py:31
  244.0 16.2 %collective-permute-done.2 = bf16[1,225,2048]{2,1,0:T(8,128)(2,1)S(1)} collective-permute-done((bf16[1,225,2048]{2,1,0:T(8,128)(2,1)S(1)}, bf16[1,225,2048]{2,1,0:T(8,128)(2,1)S(1)}, u32[]{:S(2)}, u32[]{:S(2)}) %collective-permute-start.2) | collective-permute-done | bytes 921632 | tf_op jit(solution)/shard_map/ppermute | solution.py:31
  (75 shorter events, 51.6 us)
Async XLA Ops:
  0.0 187.7 %copy-start = (f32[64,2048]{1,0:T(8,128)S(1)}, f32[64,2048]{1,0:T(8,128)}, u32[]{:S(2)}) copy-start(f32[64,2048]{1,0:T(8,128)} %param.16) | copy-start | bytes 1572868
  1.4 16.8 %copy-start.4 = (bf16[1,225,2048]{2,1,0:T(8,128)(2,1)S(1)}, bf16[1,225,2048]{2,1,0:T(8,128)(2,1)}, u32[]{:S(2)}) copy-start(bf16[1,225,2048]{2,1,0:T(8,128)(2,1)} %param.13) | copy-start | bytes 2764804
  2.8 37.6 %all-to-all-start.1 = ((bf16[225,16,1,128]{3,0,2,1:T(8,128)(2,1)}), bf16[225,16,1,128]{3,0,2,1:T(8,128)(2,1)S(1)}, u32[]{:S(2)}, u32[]{:S(2)}) async-start(bf16[225,16,1,128]{3,0,2,1:T(8,128)(2,1)} %copy.24), calls=%async_computation.1 | async-start | bytes 1900544 | tf_op jit(solution)/shard_map/all_to_all | solution.py:106
  18.4 33.6 %copy-start.5 = (bf16[1,225,2048]{2,1,0:T(8,128)(2,1)S(1)}, bf16[1,225,2048]{2,1,0:T(8,128)(2,1)}, u32[]{:S(2)}) copy-start(bf16[1,225,2048]{2,1,0:T(8,128)(2,1)} %param.11) | copy-start | bytes 2764804
  40.5 34.7 %all-to-all-start.2 = ((bf16[225,16,1,128]{3,0,2,1:T(8,128)(2,1)}), bf16[225,16,1,128]{3,0,2,1:T(8,128)(2,1)S(1)}, u32[]{:S(2)}, u32[]{:S(2)}) async-start(bf16[225,16,1,128]{3,0,2,1:T(8,128)(2,1)} %copy.25), calls=%async_computation.2 | async-start | bytes 1900544 | tf_op jit(solution)/shard_map/all_to_all | solution.py:109
  52.3 33.5 %copy-start.7 = (s32[1,2]{1,0:T(1,128)S(1)}, s32[1,2]{1,0:T(1,128)}, u32[]{:S(2)}) copy-start(s32[1,2]{1,0:T(1,128)} %param.15) | copy-start | bytes 28
  75.2 25.7 %copy-start.1 = (bf16[225,16,1,128]{3,0,2,1:T(8,128)(2,1)}, bf16[225,16,1,128]{3,0,2,1:T(8,128)(2,1)S(1)}, u32[]{:S(2)}) copy-start(bf16[225,16,1,128]{3,0,2,1:T(8,128)(2,1)S(1)} %all-to-all-done.2) | copy-start | bytes 2764804
  75.2 33.0 %all-to-all-start = ((bf16[225,16,1,128]{3,0,2,1:T(8,128)(2,1)}), bf16[225,16,1,128]{3,0,2,1:T(8,128)(2,1)S(1)}, u32[]{:S(2)}, u32[]{:S(2)}) async-start(bf16[225,16,1,128]{3,0,2,1:T(8,128)(2,1)} %copy.23), calls=%async_computation | async-start | bytes 1900544 | tf_op jit(solution)/shard_map/all_to_all | solution.py:103
  92.9 50.1 %collective-permute-start = (bf16[2,1,3600,1,128]{4,2,0,3,1:T(8,128)(2,1)}, bf16[2,1,3600,1,128]{4,2,0,3,1:T(8,128)(2,1)}, u32[]{:S(2)}, u32[]{:S(2)}) collective-permute-start(bf16[2,1,3600,1,128]{4,2,0,3,1:T(8,128)(2,1)} %maximum_bitcast_fusion), channel_id=1, source_target_pairs={{0,16},{16,32},{32,48},{48,64},{64,80},{80,96},{96,112},{112,128},... | collective-permute-start | bytes 5529608 | tf_op jit(solution)/shard_map/ppermute | solution.py:22
  100.9 42.1 %collective-permute-start.1 = (bf16[2,1,3600,1,128]{4,2,0,3,1:T(8,128)(2,1)}, bf16[2,1,3600,1,128]{4,2,0,3,1:T(8,128)(2,1)}, u32[]{:S(2)}, u32[]{:S(2)}) collective-permute-start(bf16[2,1,3600,1,128]{4,2,0,3,1:T(8,128)(2,1)} %maximum_bitcast_fusion), channel_id=1, source_target_pairs={{16,0},{32,16},{48,32},{64,48},{80,64},{96,80},{112,96},{128,112},... | collective-permute-start | bytes 5529608 | tf_op jit(solution)/shard_map/ppermute | solution.py:23
  109.9 1.6 copy-start.6
  115.4 1.6 copy-start.6
  120.8 1.6 copy-start.6
  126.2 1.6 copy-start.6
  131.7 1.6 copy-start.6
  137.1 1.6 copy-start.6
  175.2 38.4 %all-to-all-start.3 = ((bf16[16,2,14400]{2,1,0:T(2,128)(2,1)}), bf16[16,2,14400]{2,1,0:T(2,128)(2,1)S(1)}, u32[]{:S(2)}, u32[]{:S(2)}) async-start(bf16[16,2,14400]{2,1,0:T(2,128)(2,1)} %reshape.108), calls=%async_computation.3 | async-start | bytes 1851392 | tf_op jit(solution)/shard_map/all_to_all | solution.py:126
  238.6 1.2 copy-start.2
  238.9 21.3 %copy-start.3 = (bf16[225,2048]{1,0:T(8,128)(2,1)S(1)}, bf16[225,2048]{1,0:T(8,128)(2,1)}, u32[]{:S(2)}) copy-start(bf16[225,2048]{1,0:T(8,128)(2,1)} %param.17) | copy-start | bytes 2764804
  240.1 20.0 %collective-permute-start.2 = (bf16[1,225,2048]{2,1,0:T(8,128)(2,1)S(1)}, bf16[1,225,2048]{2,1,0:T(8,128)(2,1)S(1)}, u32[]{:S(2)}, u32[]{:S(2)}) collective-permute-start(bf16[1,225,2048]{2,1,0:T(8,128)(2,1)S(1)} %fusion.32), channel_id=1, source_target_pairs={{16,0},{32,16},{48,32},{64,48},{80,64},{96,80},{112,96},{128,112},... | collective-permute-start | bytes 2764808 | tf_op jit(solution)/shard_map/ppermute | solution.py:31
where the time goes:
time: 264 us; the launch traced here: 261 us
  waiting for transfers between devices  86.4 us (33%)
  starting transfers between devices  63.3 us (24%)
  other arithmetic  41.7 us (16%)
  matrix products  37.4 us (14%)
  local copies, waits for them, and re-layouts  30.6 us (12%)
    all_to_all x1, waiting for transfers between devices, on_device(): lax.all_to_all(exchanged, 'space', split_axis=0, concat_axis=1, tiled=True)  25.6 us
    all_to_all x1, waiting for transfers between devices, on_device(): lax.all_to_all(head_values[0].reshape(split_shape), 'space', split_axis=1...  21.6 us
    all_to_all x1, waiting for transfers between devices, on_device(): lax.all_to_all(head_keys[0].reshape(split_shape), 'space', split_axis=1,...  20.7 us
    all_to_all x1, other arithmetic, on_device(): lax.all_to_all(exchanged, 'space', split_axis=0, concat_axis=1, tiled=True)  20 us
    ppermute x1, waiting for transfers between devices, from_behind(): return lax.ppermute(block, axis, route)  16.2 us
    all_to_all x1, starting transfers between devices, on_device(): lax.all_to_all(head_keys[0].reshape(split_shape), 'space', split_axis=1,...  15.4 us
    dot_general x6, matrix products, one_block(): jnp.einsum('hqk,khd->qhd', weights, value_part, preferred_element_type=jn...  13.9 us
    all_to_all x1, starting transfers between devices, on_device(): lax.all_to_all(exchanged, 'space', split_axis=0, concat_axis=1, tiled=True)  11.9 us
  transfers between devices with their start and end apart: 7, of which 5 were waited for; matrix products, arithmetic and copies ran while one was open for 18% of the time, Pallas kernels for 0%

commit v1 on v0

v1 whole, which is shorter than its diff:
```python
import functools
import math

import jax
import jax.numpy as jnp
from jax import lax
from jax.experimental import pallas as pl
from jax.experimental.pallas import tpu as pltpu
from jax.sharding import PartitionSpec as P

HEAD_DIM = 128
SCALE = 1.0 / math.sqrt(HEAD_DIM)
LOG2E = 1.4426950408889634
MASKED = -1e30
MIB = 1024 * 1024


def pack_kernel(q_ref, k_ref, v_ref, out_ref, *, main):
    for part, ref in enumerate((q_ref, k_ref, v_ref)):
        out_ref[0, part * main : (part + 1) * main, :] = ref[0, :main, :]
    row = lax.broadcasted_iota(jnp.int32, (16, HEAD_DIM), 0)
    tail = jnp.zeros((16, HEAD_DIM), jnp.float32)
    for part, ref in enumerate((q_ref, k_ref, v_ref)):
        last = ref[0, main : main + 1, :].astype(jnp.float32)
        tail = jnp.where(row == part, last, tail)
    out_ref[0, 3 * main :, :] = tail.astype(jnp.bfloat16)


def pack(queries, keys, values):
    _, rows, channels = queries.shape
    heads = channels // HEAD_DIM
    main = rows - 1
    total = 3 * main + 16
    spec = pl.BlockSpec((1, rows, HEAD_DIM), lambda h: (0, 0, h))
    return pl.pallas_call(
        functools.partial(pack_kernel, main=main),
        grid=(heads,),
        in_specs=[spec] * 3,
        out_specs=pl.BlockSpec((1, total, HEAD_DIM), lambda h: (h, 0, 0)),
        out_shape=jax.ShapeDtypeStruct((heads, total, HEAD_DIM), jnp.bfloat16),
        cost_estimate=pl.CostEstimate(flops=0, bytes_accessed=6 * queries.size * 2, transcendentals=0),
        name="pack",
    )(queries, keys, values)


def attend_kernel(got_ref, out_ref, q_all, k_all, v_all, o_all, *, sources, main, block):
    row = lax.broadcasted_iota(jnp.int32, (16, HEAD_DIM), 0)
    tails = [jnp.zeros((16, HEAD_DIM), jnp.float32) for _ in range(3)]
    for s in range(sources):
        at = slice(s * main, (s + 1) * main)
        q_all[at, :] = got_ref[s, :main, :]
        k_all[at, :] = got_ref[s, main : 2 * main, :]
        v_all[at, :HEAD_DIM] = got_ref[s, 2 * main : 3 * main, :]
        tail = got_ref[s, 3 * main :, :].astype(jnp.float32)
        for part in range(3):
            tails[part] = jnp.where(row == s, tail[part : part + 1, :], tails[part])
    end = sources * main
    q_all[end:, :] = tails[0].astype(jnp.bfloat16)
    k_all[end:, :] = tails[1].astype(jnp.bfloat16)
    v_all[end:, :HEAD_DIM] = tails[2].astype(jnp.bfloat16)
    v_all[:, HEAD_DIM:] = jnp.ones((end + 16, HEAD_DIM), jnp.bfloat16)

    def one_block(i, carry):
        rows = pl.ds(pl.multiple_of(i * block, 16), block)
        scores = lax.dot_general(
            q_all[rows, :], k_all[...], (((1,), (1,)), ((), ())), preferred_element_type=jnp.float32
        )
        top = jnp.max(scores, axis=1, keepdims=True)
        weights = jnp.exp2((scores - top) * (SCALE * LOG2E)).astype(jnp.bfloat16)
        summed = jnp.dot(weights, v_all[...], preferred_element_type=jnp.float32)
        o_all[rows, :] = (summed[:, :HEAD_DIM] / summed[:, HEAD_DIM:]).astype(jnp.bfloat16)
        return carry

    lax.fori_loop(0, (end + 16) // block, one_block, 0)
    last = o_all[end:, :].astype(jnp.float32)
    for s in range(sources):
        out_ref[s, :main, :] = o_all[s * main : (s + 1) * main, :]
        out_ref[s, main : main + 1, :] = last[s : s + 1, :].astype(jnp.bfloat16)


def attend(got, rows):
    sources, total, _ = got.shape
    main = rows - 1
    tokens = sources * rows
    block = 400
    return pl.pallas_call(
        functools.partial(attend_kernel, sources=sources, main=main, block=block),
        in_specs=[pl.BlockSpec(memory_space=pltpu.VMEM)],
        out_specs=pl.BlockSpec(memory_space=pltpu.VMEM),
        out_shape=jax.ShapeDtypeStruct((sources, rows, HEAD_DIM), jnp.bfloat16),
        scratch_shapes=[
            pltpu.VMEM((tokens, HEAD_DIM), jnp.bfloat16),
            pltpu.VMEM((tokens, HEAD_DIM), jnp.bfloat16),
            pltpu.VMEM((tokens, 2 * HEAD_DIM), jnp.bfloat16),
            pltpu.VMEM((tokens, HEAD_DIM), jnp.bfloat16),
        ],
        compiler_params=pltpu.CompilerParams(vmem_limit_bytes=48 * MIB),
        cost_estimate=pl.CostEstimate(
            flops=4 * tokens * tokens * HEAD_DIM, bytes_accessed=8 * tokens * HEAD_DIM, transcendentals=tokens * tokens
        ),
        name="attend",
    )(got)


def temporal_kernel(usable_ref, q_ref, k0, k1, k2, v0, v1, v2, out_ref):
    q = q_ref[0].astype(jnp.float32)
    scores = []
    for j, ref in enumerate((k0, k1, k2)):
        score = jnp.sum(q * ref[0].astype(jnp.float32), axis=1, keepdims=True) * SCALE
        scores.append(jnp.where(usable_ref[j] > 0, score, MASKED))
    top = jnp.maximum(jnp.maximum(scores[0], scores[1]), scores[2])
    terms = [jnp.exp(score - top) for score in scores]
    total = terms[0] + terms[1] + terms[2]
    summed = jnp.zeros_like(q)
    for term, ref in zip(terms, (v0, v1, v2)):
        summed += term.astype(jnp.bfloat16).astype(jnp.float32) * ref[0].astype(jnp.float32)
    out_ref[0] = summed / total


def temporal_attend(usable, queries, near_keys, near_values):
    _, rows, channels = queries.shape
    spec = pl.BlockSpec((1, rows, HEAD_DIM), lambda h: (0, 0, h))
    return pl.pallas_call(
        temporal_kernel,
        grid=(channels // HEAD_DIM,),
        in_specs=[pl.BlockSpec(memory_space=pltpu.SMEM)] + [spec] * 7,
        out_specs=spec,
        out_shape=jax.ShapeDtypeStruct(queries.shape, jnp.float32),
        cost_estimate=pl.CostEstimate(flops=12 * queries.size, bytes_accessed=18 * queries.size, transcendentals=0),
        name="temporal",
    )(usable, queries, *near_keys, *near_values)


def finish_kernel(first_ref, spatial_ref, temporal_ref, residual_ref, gate_ref, fresh_ref, out_ref):
    mixed = (spatial_ref[0].astype(jnp.float32) + temporal_ref[0]).astype(jnp.bfloat16)
    updated = residual_ref[0].astype(jnp.float32) + gate_ref[...] * mixed.astype(jnp.float32)
    is_first = first_ref[0] > 0
    out_ref[0] = jnp.where(is_first, fresh_ref[...].astype(jnp.float32), updated).astype(jnp.bfloat16)


def finish(is_first, spatial, temporal, residual, gate_row, fresh):
    heads, rows, _ = spatial.shape
    by_head = pl.BlockSpec((1, rows, HEAD_DIM), lambda h: (0, 0, h))
    return pl.pallas_call(
        finish_kernel,
        grid=(heads,),
        in_specs=[
            pl.BlockSpec(memory_space=pltpu.SMEM),
            pl.BlockSpec((1, rows, HEAD_DIM), lambda h: (h, 0, 0)),
            by_head,
            by_head,
            pl.BlockSpec((1, HEAD_DIM), lambda h: (0, h)),
            pl.BlockSpec((rows, HEAD_DIM), lambda h: (0, h)),
        ],
        out_specs=by_head,
        out_shape=jax.ShapeDtypeStruct(residual.shape, jnp.bfloat16),
        cost_estimate=pl.CostEstimate(flops=4 * residual.size, bytes_accessed=12 * residual.size, transcendentals=0),
        name="finish",
    )(is_first, spatial, temporal, residual, gate_row, fresh)


def on_device(residual, head_queries, head_keys, head_values, levels, window, level_gate, fresh_frame):
    rows = head_queries.shape[1]
    frame = lax.axis_index("queue")
    frames = lax.axis_size("queue")
    up = [(i, i + 1) for i in range(frames - 1)]
    down = [(j, i) for i, j in up]

    sent = pack(head_queries, head_keys, head_values)
    got = lax.all_to_all(sent, "space", split_axis=0, concat_axis=0, tiled=True)

    near_keys = (lax.ppermute(head_keys, "queue", up), head_keys, lax.ppermute(head_keys, "queue", down))
    near_values = (lax.ppermute(head_values, "queue", up), head_values, lax.ppermute(head_values, "queue", down))
    before = (window[0, 0] >= 1) & (frame >= 1)
    after = (window[0, 1] >= 1) & (frame <= frames - 2)
    usable = jnp.stack([before, jnp.bool_(True), after]).astype(jnp.int32)
    temporal = temporal_attend(usable, head_queries, near_keys, near_values)

    back = attend(got, rows)
    spatial = lax.all_to_all(back, "space", split_axis=0, concat_axis=0, tiled=True)
    gate_row = lax.dynamic_slice_in_dim(level_gate, levels[0], 1, axis=0)
    is_first = (frame == 0).astype(jnp.int32)[None]
    updated = finish(is_first, spatial, temporal, residual, gate_row, fresh_frame)
    return lax.ppermute(updated, "queue", [(i, (i - 1) % frames) for i in range(frames)])


def solution(mesh):
    placed = (
        P("queue", "space", None),
        P("queue", "space", None),
        P("queue", "space", None),
        P("queue", "space", None),
        P("queue"),
        P("queue", None),
        P(),
        P("space", None),
    )
    return jax.shard_map(
        on_device, mesh=mesh, in_specs=placed, out_specs=P("queue", "space", None), check_vma=False
    )
```

time: 264 us -> 219 us (0.83)
  blocking collectives: 0 us -> 78.7 us
  Pallas kernels: 0 us -> 63.8 us
  waiting for transfers between devices: 86.4 us -> 41.4 us
  other arithmetic: 41.7 us -> 0.61 us
  matrix products: 37.4 us -> 0 us
  starting transfers between devices: 63.3 us -> 27.8 us
  local copies, waits for them, and re-layouts: 30.6 us -> 3.06 us
    all_to_all x0 -> x1, blocking collectives: none -> 78.7 us  [on_device(): got = lax.all_to_all(sent, 'space', split_axis=0, concat_axis=0, tiled=True)]
    all_to_all x4 -> x1, waiting for transfers between devices: 70.2 us -> 0.01 us  [on_device(): lax.all_to_all(back, 'space', split_axis=0, concat_axis=0, tiled=True)]
    pallas_call x0 -> x4, Pallas kernels: none -> 63.8 us  [the longest x1 32.5 us: attend(): pl.pallas_call(functools.partial(attend_kernel, sources=sources, main=mai...]
    dot_general x15 -> x0, matrix products: 37.4 us -> none  [the longest x6 13.9 us: one_block(): jnp.einsum('hqk,khd->qhd', weights, value_part, preferred_element_type=jn...]
    all_to_all x4 -> x1, starting transfers between devices: 49.4 us -> 12.2 us  [on_device(): lax.all_to_all(back, 'space', split_axis=0, concat_axis=0, tiled=True)]
    ppermute x3 -> x5, waiting for transfers between devices: 16.2 us -> 41.4 us  [the longest x1 15.5 us: on_device(): lax.ppermute(updated, 'queue', [(i, (i - 1) % frames) for i in range(fram...]
    all_to_all x1 -> x0, other arithmetic: 20 us -> none  [on_device(): lax.all_to_all(exchanged, 'space', split_axis=0, concat_axis=1, tiled=True)]
    another operation x12 -> x0, local copies, waits for them, and re-layouts: 13.8 us -> none
  transfers between devices with their start and end apart: 7 -> 6, of which waited for: 5 -> 5; matrix products, arithmetic and copies ran while one was open for 18% -> 1% of each run, Pallas kernels for 0% -> 5%
where the time goes in v1:
time: 219 us; the launch traced here: 217 us
  blocking collectives  78.7 us (36%)
  Pallas kernels  63.8 us (29%)
  waiting for transfers between devices  41.4 us (19%)
  starting transfers between devices  27.8 us (13%)
  local copies, waits for them, and re-layouts  3.06 us (1%)
    all_to_all x1, blocking collectives, on_device(): got = lax.all_to_all(sent, 'space', split_axis=0, concat_axis=0, tiled=True)  78.7 us
    pallas_call x1, Pallas kernels, attend(): pl.pallas_call(functools.partial(attend_kernel, sources=sources, main=mai...  32.5 us
    ppermute x1, waiting for transfers between devices, on_device(): lax.ppermute(updated, 'queue', [(i, (i - 1) % frames) for i in range(fram...  15.5 us
    ppermute x1, waiting for transfers between devices, on_device(): lax.ppermute(head_keys, 'queue', up)  14.1 us
    all_to_all x1, starting transfers between devices, on_device(): lax.all_to_all(back, 'space', split_axis=0, concat_axis=0, tiled=True)  12.2 us
    pallas_call x1, Pallas kernels, temporal_attend(): pl.pallas_call(temporal_kernel, grid=(channels // HEAD_DIM,), in_specs=[p...  11.9 us
    pallas_call x1, Pallas kernels, finish(): pl.pallas_call(finish_kernel, grid=(heads,), in_specs=[pl.BlockSpec(memor...  9.89 us
    pallas_call x1, Pallas kernels, pack(): pl.pallas_call(functools.partial(pack_kernel, main=main), grid=(heads,),...  9.57 us
  transfers between devices with their start and end apart: 6, of which 5 were waited for; matrix products, arithmetic and copies ran while one was open for 1% of the time, Pallas kernels for 5%

profile of v1, /device:TPU:7, one launch (start us, length us, event | category | flops | bytes accessed | tf_op | source)
XLA Modules:
  0.0 217.3 jit_solution(10774838994444800360)
XLA Ops:
  0.0 9.6 %pack.1 = bf16[16,688,128]{2,1,0:T(8,128)(2,1)} custom-call(bf16[1,225,2048]{2,1,0:T(8,128)(2,1)} %q_ref.3, bf16[1,225,2048]{2,1,0:T(8,128)(2,1)} %k1.1, bf16[1,225,2048]{2,1,0:T(8,128)(2,1)} %v1.1), custom_call_target="tpu_custom_call" | custom-call | bytes 5529600 | tf_op jit(solution)/shard_map/pack/pallas_call | solution.py:35
  9.6 78.7 %all_to_all.10.got_ref = bf16[16,688,128]{2,1,0:T(8,128)(2,1)S(1)} all-to-all(bf16[16,688,128]{2,1,0:T(8,128)(2,1)} %pack.1), channel_id=1, replica_groups=mesh['queue'=32,'space'=16] {'space'}, dimensions={0} | all-to-all | bytes 5636096 | tf_op jit(solution)/shard_map/all_to_all | solution.py:170
  88.3 32.5 %attend.1 = bf16[16,225,128]{2,1,0:T(8,128)(2,1)} custom-call(bf16[16,688,128]{2,1,0:T(8,128)(2,1)S(1)} %all_to_all.10.got_ref), custom_call_target="tpu_custom_call" | custom-call | flops 6635520000 | bytes 3686400 | tf_op jit(solution)/shard_map/attend/pallas_call | solution.py:86
  120.8 12.2 %all-to-all-start.1 = ((bf16[16,225,128]{2,1,0:T(8,128)(2,1)}), bf16[16,225,128]{2,1,0:T(8,128)(2,1)S(1)}, u32[]{:S(2)}, u32[]{:S(2)}) async-start(bf16[16,225,128]{2,1,0:T(8,128)(2,1)} %attend.1), calls=%async_computation.1 | async-start | bytes 1900544 | tf_op jit(solution)/shard_map/all_to_all | solution.py:180
  133.0 4.1 %collective-permute-start = (bf16[1,225,2048]{2,1,0:T(8,128)(2,1)S(1)}, bf16[1,225,2048]{2,1,0:T(8,128)(2,1)}, u32[]{:S(2)}, u32[]{:S(2)}) collective-permute-start(bf16[1,225,2048]{2,1,0:T(8,128)(2,1)S(1)} %copy-done.2), channel_id=1, source_target_pairs={{0,16},{16,32},{32,48},{48,64},{64,80},{80,96},{96,112},{112,128},... | collective-permute-start | bytes 2764808 | tf_op jit(solution)/shard_map/ppermute | solution.py:172
  137.1 1.9 collective-permute-start.1
  139.0 5.8 %collective-permute-start.2 = (bf16[1,225,2048]{2,1,0:T(8,128)(2,1)S(1)}, bf16[1,225,2048]{2,1,0:T(8,128)(2,1)}, u32[]{:S(2)}, u32[]{:S(2)}) collective-permute-start(bf16[1,225,2048]{2,1,0:T(8,128)(2,1)S(1)} %copy-done.3), channel_id=1, source_target_pairs={{0,16},{16,32},{32,48},{48,64},{64,80},{80,96},{96,112},{112,128},... | collective-permute-start | bytes 2764808 | tf_op jit(solution)/shard_map/ppermute | solution.py:173
  144.8 1.9 collective-permute-start.3
  146.7 0.6 fusion
  149.2 0.6 add_convert_fusion.usable_ref
  149.8 0.0 copy-done
  149.8 0.6 constant_dynamic-slice_fusion.gate_ref
  150.4 14.1 %collective-permute-done.k0 = bf16[1,225,2048]{2,1,0:T(8,128)(2,1)} collective-permute-done((bf16[1,225,2048]{2,1,0:T(8,128)(2,1)S(1)}, bf16[1,225,2048]{2,1,0:T(8,128)(2,1)}, u32[]{:S(2)}, u32[]{:S(2)}) %collective-permute-start) | collective-permute-done | bytes 921632 | tf_op jit(solution)/shard_map/ppermute | solution.py:172
  164.5 1.6 collective-permute-done.1.k2
  166.1 8.6 %collective-permute-done.2.v0 = bf16[1,225,2048]{2,1,0:T(8,128)(2,1)} collective-permute-done((bf16[1,225,2048]{2,1,0:T(8,128)(2,1)S(1)}, bf16[1,225,2048]{2,1,0:T(8,128)(2,1)}, u32[]{:S(2)}, u32[]{:S(2)}) %collective-permute-start.2) | collective-permute-done | bytes 921632 | tf_op jit(solution)/shard_map/ppermute | solution.py:173
  174.7 1.6 collective-permute-done.3.v2
  176.3 11.9 %temporal.1.temporal_ref = f32[1,225,2048]{2,1,0:T(8,128)} custom-call(s32[3]{0:T(128)} %add_convert_fusion.usable_ref, bf16[1,225,2048]{2,1,0:T(8,128)(2,1)} %q_ref.3, bf16[1,225,2048]{2,1,0:T(8,128)(2,1)} %collective-permute-done.k0, bf16[1,225,2048]{2,1,0:T(8,128)(2,1)} %k1.1, bf16[1,225,2048]{2,1,0:T(8,128)(2,1)} %collective-permute-done.1.k2, ...), custom_call_target="tpu_custom_call" | custom-call | flops 5529600 | bytes 8294400 | tf_op jit(solution)/shard_map/temporal/pallas_call | solution.py:123
  188.2 0.0 all-to-all-done.1.spatial_ref
  188.2 0.0 copy-start.1
  188.2 0.9 copy-done.1
  189.1 9.9 %finish.1 = bf16[1,225,2048]{2,1,0:T(8,128)(2,1)} custom-call(s32[1]{0:T(128)} %bitcast.first_ref, bf16[16,225,128]{2,1,0:T(8,128)(2,1)} %copy-done.1, f32[1,225,2048]{2,1,0:T(8,128)} %temporal.1.temporal_ref, bf16[1,225,2048]{2,1,0:T(8,128)(2,1)} %residual_ref.1, f32[1,2048]{1,0:T(1,128)} %constant_dynamic-slice_fusion.gate_ref, bf16[225,2048]{1,0:T(8,128)(2,1)} %fresh_ref.1), custom_call_target="tpu_custom_call" | custom-call | flops 1843200 | bytes 5529600 | tf_op jit(solution)/shard_map/finish/pallas_call | solution.py:144
  199.0 1.9 collective-permute-start.4
  200.9 15.5 %collective-permute-done.4 = bf16[1,225,2048]{2,1,0:T(8,128)(2,1)S(1)} collective-permute-done((bf16[1,225,2048]{2,1,0:T(8,128)(2,1)}, bf16[1,225,2048]{2,1,0:T(8,128)(2,1)S(1)}, u32[]{:S(2)}, u32[]{:S(2)}) %collective-permute-start.4) | collective-permute-done | bytes 921632 | tf_op jit(solution)/shard_map/ppermute | solution.py:184
  216.4 0.9 copy.11
  (7 shorter events, 0.0 us)
Async XLA Ops:
  0.0 149.8 %copy-start = (f32[64,2048]{1,0:T(8,128)S(1)}, f32[64,2048]{1,0:T(8,128)}, u32[]{:S(2)}) copy-start(f32[64,2048]{1,0:T(8,128)} %param.14) | copy-start | bytes 1572868
  88.3 44.7 %copy-start.2 = (bf16[1,225,2048]{2,1,0:T(8,128)(2,1)S(1)}, bf16[1,225,2048]{2,1,0:T(8,128)(2,1)}, u32[]{:S(2)}) copy-start(bf16[1,225,2048]{2,1,0:T(8,128)(2,1)} %k1.1) | copy-start | bytes 2764804
  88.3 50.7 %copy-start.3 = (bf16[1,225,2048]{2,1,0:T(8,128)(2,1)S(1)}, bf16[1,225,2048]{2,1,0:T(8,128)(2,1)}, u32[]{:S(2)}) copy-start(bf16[1,225,2048]{2,1,0:T(8,128)(2,1)} %v1.1) | copy-start | bytes 2764804
  88.3 58.4 %copy-start.4 = (s32[1,2]{1,0:T(1,128)S(1)}, s32[1,2]{1,0:T(1,128)}, u32[]{:S(2)}) copy-start(s32[1,2]{1,0:T(1,128)} %param.13) | copy-start | bytes 28
  120.8 67.4 %all-to-all-start.1 = ((bf16[16,225,128]{2,1,0:T(8,128)(2,1)}), bf16[16,225,128]{2,1,0:T(8,128)(2,1)S(1)}, u32[]{:S(2)}, u32[]{:S(2)}) async-start(bf16[16,225,128]{2,1,0:T(8,128)(2,1)} %attend.1), calls=%async_computation.1 | async-start | bytes 1900544 | tf_op jit(solution)/shard_map/all_to_all | solution.py:180
  133.0 31.5 %collective-permute-start = (bf16[1,225,2048]{2,1,0:T(8,128)(2,1)S(1)}, bf16[1,225,2048]{2,1,0:T(8,128)(2,1)}, u32[]{:S(2)}, u32[]{:S(2)}) collective-permute-start(bf16[1,225,2048]{2,1,0:T(8,128)(2,1)S(1)} %copy-done.2), channel_id=1, source_target_pairs={{0,16},{16,32},{32,48},{48,64},{64,80},{80,96},{96,112},{112,128},... | collective-permute-start | bytes 2764808 | tf_op jit(solution)/shard_map/ppermute | solution.py:172
  137.1 29.0 %collective-permute-start.1 = (bf16[1,225,2048]{2,1,0:T(8,128)(2,1)S(1)}, bf16[1,225,2048]{2,1,0:T(8,128)(2,1)}, u32[]{:S(2)}, u32[]{:S(2)}) collective-permute-start(bf16[1,225,2048]{2,1,0:T(8,128)(2,1)S(1)} %copy-done.2), channel_id=1, source_target_pairs={{16,0},{32,16},{48,32},{64,48},{80,64},{96,80},{112,96},{128,112},... | collective-permute-start | bytes 2764808 | tf_op jit(solution)/shard_map/ppermute | solution.py:172
  139.0 35.7 %collective-permute-start.2 = (bf16[1,225,2048]{2,1,0:T(8,128)(2,1)S(1)}, bf16[1,225,2048]{2,1,0:T(8,128)(2,1)}, u32[]{:S(2)}, u32[]{:S(2)}) collective-permute-start(bf16[1,225,2048]{2,1,0:T(8,128)(2,1)S(1)} %copy-done.3), channel_id=1, source_target_pairs={{0,16},{16,32},{32,48},{48,64},{64,80},{80,96},{96,112},{112,128},... | collective-permute-start | bytes 2764808 | tf_op jit(solution)/shard_map/ppermute | solution.py:173
  144.8 31.5 %collective-permute-start.3 = (bf16[1,225,2048]{2,1,0:T(8,128)(2,1)S(1)}, bf16[1,225,2048]{2,1,0:T(8,128)(2,1)}, u32[]{:S(2)}, u32[]{:S(2)}) collective-permute-start(bf16[1,225,2048]{2,1,0:T(8,128)(2,1)S(1)} %copy-done.3), channel_id=1, source_target_pairs={{16,0},{32,16},{48,32},{64,48},{80,64},{96,80},{112,96},{128,112},... | collective-permute-start | bytes 2764808 | tf_op jit(solution)/shard_map/ppermute | solution.py:173
  188.2 0.9 copy-start.1
  199.0 17.4 %collective-permute-start.4 = (bf16[1,225,2048]{2,1,0:T(8,128)(2,1)}, bf16[1,225,2048]{2,1,0:T(8,128)(2,1)S(1)}, u32[]{:S(2)}, u32[]{:S(2)}) collective-permute-start(bf16[1,225,2048]{2,1,0:T(8,128)(2,1)} %finish.1), channel_id=1, source_target_pairs={{0,496},{16,0},{32,16},{48,32},{64,48},{80,64},{96,80},{112,96},{1... | collective-permute-start | bytes 2764808 | tf_op jit(solution)/shard_map/ppermute | solution.py:184

commit v2 on v1

v2 whole, which is shorter than its diff:
```python
import functools
import math

import jax
import jax.numpy as jnp
from jax import lax
from jax.experimental import pallas as pl
from jax.experimental.pallas import tpu as pltpu
from jax.sharding import PartitionSpec as P

HEAD_DIM = 128
SCALE = 1.0 / math.sqrt(HEAD_DIM)
LOG2E = 1.4426950408889634
MASKED = -1e30
MIB = 1024 * 1024
STEP_HEADS = 4
QUERY_BLOCK = 720
KEY_BLOCK = 720


def columns(head):
    return slice(head * HEAD_DIM, (head + 1) * HEAD_DIM)


def pack_kernel(q_ref, k_ref, v_ref, out_ref, own_ref, *, main):
    for part, ref in enumerate((k_ref, v_ref)):
        own_ref[part, main:, :] = jnp.zeros_like(own_ref[part, main:, :])
        own_ref[part, : main + 1, :] = ref[0]
    row = lax.broadcasted_iota(jnp.int32, (16, HEAD_DIM), 0)
    for head in range(STEP_HEADS):
        tail = jnp.zeros((16, HEAD_DIM), jnp.float32)
        for part, ref in enumerate((q_ref, k_ref, v_ref)):
            out_ref[head, part * main : (part + 1) * main, :] = ref[0, :main, columns(head)]
            last = ref[0, main : main + 1, columns(head)].astype(jnp.float32)
            tail = jnp.where(row == part, last, tail)
        out_ref[head, 3 * main :, :] = tail.astype(jnp.bfloat16)


def pack(queries, keys, values):
    _, rows, channels = queries.shape
    heads = channels // HEAD_DIM
    main = rows - 1
    total = 3 * main + 16
    spec = pl.BlockSpec((1, rows, STEP_HEADS * HEAD_DIM), lambda h: (0, 0, h))
    return pl.pallas_call(
        functools.partial(pack_kernel, main=main),
        grid=(heads // STEP_HEADS,),
        in_specs=[spec] * 3,
        out_specs=[
            pl.BlockSpec((STEP_HEADS, total, HEAD_DIM), lambda h: (h, 0, 0)),
            pl.BlockSpec((2, main + 16, STEP_HEADS * HEAD_DIM), lambda h: (0, 0, h)),
        ],
        out_shape=[
            jax.ShapeDtypeStruct((heads, total, HEAD_DIM), jnp.bfloat16),
            jax.ShapeDtypeStruct((2, main + 16, channels), jnp.bfloat16),
        ],
        cost_estimate=pl.CostEstimate(flops=0, bytes_accessed=8 * queries.size * 2, transcendentals=0),
        name="pack",
    )(queries, keys, values)


def attend_kernel(got_ref, out_ref, q_all, k_all, v_all, o_all, *, sources, main):
    row = lax.broadcasted_iota(jnp.int32, (16, HEAD_DIM), 0)
    tails = [jnp.zeros((16, HEAD_DIM), jnp.float32) for _ in range(3)]
    for s in range(sources):
        at = slice(s * main, (s + 1) * main)
        q_all[at, :] = got_ref[s, :main, :]
        k_all[at, :] = got_ref[s, main : 2 * main, :]
        v_all[at, :HEAD_DIM] = got_ref[s, 2 * main : 3 * main, :]
        tail = got_ref[s, 3 * main :, :].astype(jnp.float32)
        for part in range(3):
            tails[part] = jnp.where(row == s, tail[part : part + 1, :], tails[part])
    end = sources * main
    q_all[end:, :] = tails[0].astype(jnp.bfloat16)
    k_all[end:, :] = tails[1].astype(jnp.bfloat16)
    v_all[end:, :HEAD_DIM] = tails[2].astype(jnp.bfloat16)
    v_all[:, HEAD_DIM:] = jnp.ones((end + 16, HEAD_DIM), jnp.bfloat16)

    def one_block(i, carry):
        rows = pl.ds(pl.multiple_of(i * QUERY_BLOCK, 16), QUERY_BLOCK)
        queries = q_all[rows, :]
        top = summed = None
        for start in range(0, end + 16, KEY_BLOCK):
            keys = slice(start, start + KEY_BLOCK)
            scores = lax.dot_general(
                queries, k_all[keys, :], (((1,), (1,)), ((), ())), preferred_element_type=jnp.float32
            )
            here = jnp.max(scores, axis=1, keepdims=True)
            new_top = here if top is None else jnp.maximum(top, here)
            weights = jnp.exp2((scores - new_top) * (SCALE * LOG2E)).astype(jnp.bfloat16)
            part = jnp.dot(weights, v_all[keys, :], preferred_element_type=jnp.float32)
            summed = part if top is None else summed * jnp.exp2((top - new_top) * (SCALE * LOG2E)) + part
            top = new_top
        o_all[rows, :] = (summed[:, :HEAD_DIM] / summed[:, HEAD_DIM:]).astype(jnp.bfloat16)
        return carry

    lax.fori_loop(0, (end + 16) // QUERY_BLOCK, one_block, 0, unroll=True)
    last = o_all[end:, :].astype(jnp.float32)
    for s in range(sources):
        out_ref[s, :main, :] = o_all[s * main : (s + 1) * main, :]
        out_ref[s, main : main + 1, :] = last[s : s + 1, :].astype(jnp.bfloat16)


def attend(got, rows):
    sources, total, _ = got.shape
    main = rows - 1
    tokens = sources * rows
    return pl.pallas_call(
        functools.partial(attend_kernel, sources=sources, main=main),
        in_specs=[pl.BlockSpec(memory_space=pltpu.VMEM)],
        out_specs=pl.BlockSpec(memory_space=pltpu.VMEM),
        out_shape=jax.ShapeDtypeStruct((sources, rows, HEAD_DIM), jnp.bfloat16),
        scratch_shapes=[
            pltpu.VMEM((tokens, HEAD_DIM), jnp.bfloat16),
            pltpu.VMEM((tokens, HEAD_DIM), jnp.bfloat16),
            pltpu.VMEM((tokens, 2 * HEAD_DIM), jnp.bfloat16),
            pltpu.VMEM((tokens, HEAD_DIM), jnp.bfloat16),
        ],
        compiler_params=pltpu.CompilerParams(vmem_limit_bytes=48 * MIB),
        cost_estimate=pl.CostEstimate(
            flops=4 * tokens * tokens * HEAD_DIM, bytes_accessed=8 * tokens * HEAD_DIM, transcendentals=tokens * tokens
        ),
        name="attend",
    )(got)


def temporal_kernel(usable_ref, q_ref, k_ref, v_ref, before_ref, after_ref, out_ref):
    rows = q_ref.shape[1]
    for head in range(STEP_HEADS):
        at = columns(head)
        q = q_ref[0, :, at].astype(jnp.float32)
        keys = (before_ref[0, :rows, at], k_ref[0, :, at], after_ref[0, :rows, at])
        values = (before_ref[1, :rows, at], v_ref[0, :, at], after_ref[1, :rows, at])
        scores = []
        for j in range(3):
            score = jnp.sum(q * keys[j].astype(jnp.float32), axis=1, keepdims=True) * SCALE
            scores.append(jnp.where(usable_ref[j] > 0, score, MASKED))
        top = jnp.maximum(jnp.maximum(scores[0], scores[1]), scores[2])
        terms = [jnp.exp(score - top) for score in scores]
        total = terms[0] + terms[1] + terms[2]
        summed = jnp.zeros_like(q)
        for j in range(3):
            summed += terms[j].astype(jnp.bfloat16).astype(jnp.float32) * values[j].astype(jnp.float32)
        out_ref[0, :, at] = summed / total


def temporal_attend(usable, queries, keys, values, before, after):
    _, rows, channels = queries.shape
    width = STEP_HEADS * HEAD_DIM
    spec = pl.BlockSpec((1, rows, width), lambda h: (0, 0, h))
    pair = pl.BlockSpec((2, before.shape[1], width), lambda h: (0, 0, h))
    return pl.pallas_call(
        temporal_kernel,
        grid=(channels // width,),
        in_specs=[pl.BlockSpec(memory_space=pltpu.SMEM), spec, spec, spec, pair, pair],
        out_specs=spec,
        out_shape=jax.ShapeDtypeStruct(queries.shape, jnp.float32),
        cost_estimate=pl.CostEstimate(flops=12 * queries.size, bytes_accessed=18 * queries.size, transcendentals=0),
        name="temporal",
    )(usable, queries, keys, values, before, after)


def finish_kernel(first_ref, spatial_ref, temporal_ref, residual_ref, gate_ref, fresh_ref, out_ref):
    is_first = first_ref[0] > 0
    for head in range(STEP_HEADS):
        at = columns(head)
        mixed = (spatial_ref[head].astype(jnp.float32) + temporal_ref[0, :, at]).astype(jnp.bfloat16)
        updated = residual_ref[0, :, at].astype(jnp.float32) + gate_ref[:, at] * mixed.astype(jnp.float32)
        fresh = fresh_ref[:, at].astype(jnp.float32)
        out_ref[0, :, at] = jnp.where(is_first, fresh, updated).astype(jnp.bfloat16)


def finish(is_first, spatial, temporal, residual, gate_row, fresh):
    heads, rows, _ = spatial.shape
    width = STEP_HEADS * HEAD_DIM
    by_head = pl.BlockSpec((1, rows, width), lambda h: (0, 0, h))
    return pl.pallas_call(
        finish_kernel,
        grid=(heads // STEP_HEADS,),
        in_specs=[
            pl.BlockSpec(memory_space=pltpu.SMEM),
            pl.BlockSpec((STEP_HEADS, rows, HEAD_DIM), lambda h: (h, 0, 0)),
            by_head,
            by_head,
            pl.BlockSpec((1, width), lambda h: (0, h)),
            pl.BlockSpec((rows, width), lambda h: (0, h)),
        ],
        out_specs=by_head,
        out_shape=jax.ShapeDtypeStruct(residual.shape, jnp.bfloat16),
        cost_estimate=pl.CostEstimate(flops=4 * residual.size, bytes_accessed=12 * residual.size, transcendentals=0),
        name="finish",
    )(is_first, spatial, temporal, residual, gate_row, fresh)


def on_device(residual, head_queries, head_keys, head_values, levels, window, level_gate, fresh_frame):
    rows = head_queries.shape[1]
    frame = lax.axis_index("queue")
    frames = lax.axis_size("queue")
    up = [(i, i + 1) for i in range(frames - 1)]
    down = [(j, i) for i, j in up]

    sent, own = pack(head_queries, head_keys, head_values)
    got = lax.all_to_all(sent, "space", split_axis=0, concat_axis=0, tiled=True)

    before = (window[0, 0] >= 1) & (frame >= 1)
    after = (window[0, 1] >= 1) & (frame <= frames - 2)
    usable = jnp.stack([before, jnp.bool_(True), after]).astype(jnp.int32)
    gate_row = lax.dynamic_slice_in_dim(level_gate, levels[0], 1, axis=0)
    is_first = (frame == 0).astype(jnp.int32)[None]

    got, own = lax.optimization_barrier((got, own))
    from_before = lax.ppermute(own, "queue", up)
    from_after = lax.ppermute(own, "queue", down)
    back = attend(got, rows)
    back, from_before, from_after = lax.optimization_barrier((back, from_before, from_after))
    temporal = temporal_attend(usable, head_queries, head_keys, head_values, from_before, from_after)
    spatial = lax.all_to_all(back, "space", split_axis=0, concat_axis=0, tiled=True)
    updated = finish(is_first, spatial, temporal, residual, gate_row, fresh_frame)
    return lax.ppermute(updated, "queue", [(i, (i - 1) % frames) for i in range(frames)])


def solution(mesh):
    placed = (
        P("queue", "space", None),
        P("queue", "space", None),
        P("queue", "space", None),
        P("queue", "space", None),
        P("queue"),
        P("queue", None),
        P(),
        P("space", None),
    )
    return jax.shard_map(
        on_device, mesh=mesh, in_specs=placed, out_specs=P("queue", "space", None), check_vma=False
    )
```

time: 219 us -> 178 us (0.81)
  Pallas kernels: 63.8 us -> 33.9 us
  starting transfers between devices: 27.8 us -> 20.2 us
  waiting for transfers between devices: 41.4 us -> 38.9 us
    ppermute x4 -> x2, waiting for transfers between devices: 25.9 us -> 7.85 us  [the longest x1 6.61 us: on_device(): from_after = lax.ppermute(own, 'queue', down)]
    pallas_call x3, Pallas kernels: 31.3 us -> 15.6 us  [the longest x1 6.32 us: temporal_attend(): pl.pallas_call(temporal_kernel, grid=(channels // width,), in_specs=[pl.B...]
    all_to_all x1, waiting for transfers between devices: 0.01 us -> 15.5 us  [on_device(): lax.all_to_all(back, 'space', split_axis=0, concat_axis=0, tiled=True)]
    pallas_call x1, Pallas kernels: 32.5 us -> 18.4 us  [attend(): pl.pallas_call(functools.partial(attend_kernel, sources=sources, main=mai...]
    all_to_all x1, starting transfers between devices: 12.2 us -> 3.64 us  [on_device(): lax.all_to_all(back, 'space', split_axis=0, concat_axis=0, tiled=True)]
    ppermute x4 -> x2, starting transfers between devices: 13.7 us -> 14.7 us  [the longest x1 12.7 us: on_device(): from_before = lax.ppermute(own, 'queue', up)]
  transfers between devices with their start and end apart: 6 -> 4, of which waited for: 5 -> 4; matrix products, arithmetic and copies ran while one was open for 1% -> 1% of each run, Pallas kernels for 5% -> 14%
where the time goes in v2:
time: 178 us
  blocking collectives  78.8 us (44%)
  waiting for transfers between devices  38.9 us (22%)
  Pallas kernels  33.9 us (19%)
  starting transfers between devices  20.2 us (11%)
  local copies, waits for them, and re-layouts  3.09 us (2%)
  between operations  2.06 us (1%)
    all_to_all x1, blocking collectives, on_device(): got = lax.all_to_all(sent, 'space', split_axis=0, concat_axis=0, tiled=True)  78.8 us
    pallas_call x1, Pallas kernels, attend(): pl.pallas_call(functools.partial(attend_kernel, sources=sources, main=mai...  18.4 us
    all_to_all x1, waiting for transfers between devices, on_device(): lax.all_to_all(back, 'space', split_axis=0, concat_axis=0, tiled=True)  15.5 us
    ppermute x1, waiting for transfers between devices, on_device(): lax.ppermute(updated, 'queue', [(i, (i - 1) % frames) for i in range(fram...  15.5 us
    ppermute x1, starting transfers between devices, on_device(): from_before = lax.ppermute(own, 'queue', up)  12.7 us
    ppermute x1, waiting for transfers between devices, on_device(): from_after = lax.ppermute(own, 'queue', down)  6.61 us
    pallas_call x1, Pallas kernels, temporal_attend(): pl.pallas_call(temporal_kernel, grid=(channels // width,), in_specs=[pl.B...  6.32 us
    pallas_call x1, Pallas kernels, pack(): pl.pallas_call(functools.partial(pack_kernel, main=main), grid=(heads //...  4.91 us
  transfers between devices with their start and end apart: 4, of which 4 were waited for; matrix products, arithmetic and copies ran while one was open for 1% of the time, Pallas kernels for 14%

profile of v2, /device:TPU:7, one launch (start us, length us, event | category | flops | bytes accessed | tf_op | source)
XLA Modules:
  0.0 177.6 jit_solution(9411131219414113602)
XLA Ops:
  0.0 0.0 copy-start
  0.0 4.9 %pack.1 = (bf16[16,688,128]{2,1,0:T(8,128)(2,1)}, bf16[2,240,2048]{2,1,0:T(8,128)(2,1)}) custom-call(bf16[1,225,2048]{2,1,0:T(8,128)(2,1)} %q_ref.3, bf16[1,225,2048]{2,1,0:T(8,128)(2,1)} %k_ref.3, bf16[1,225,2048]{2,1,0:T(8,128)(2,1)} %v_ref.3), custom_call_target="tpu_custom_call" | custom-call | bytes 7372800 | tf_op jit(solution)/shard_map/pack/pallas_call | solution.py:45
  4.9 0.0 copy-start.4
  4.9 78.8 %all_to_all.10.got_ref = bf16[16,688,128]{2,1,0:T(8,128)(2,1)S(1)} all-to-all(bf16[16,688,128]{2,1,0:T(8,128)(2,1)} %get-tuple-element.12), channel_id=1, replica_groups=mesh['queue'=32,'space'=16] {'space'}, dimensions={0} | all-to-all | bytes 5636096 | tf_op jit(solution)/shard_map/all_to_all | solution.py:203
  83.8 0.0 copy-done.4
  83.8 12.7 %collective-permute-start = (bf16[2,240,2048]{2,1,0:T(8,128)(2,1)S(1)}, bf16[2,240,2048]{2,1,0:T(8,128)(2,1)S(1)}, u32[]{:S(2)}, u32[]{:S(2)}) collective-permute-start(bf16[2,240,2048]{2,1,0:T(8,128)(2,1)S(1)} %copy-done.4), channel_id=1, source_target_pairs={{0,16},{16,32},{32,48},{48,64},{64,80},{80,96},{96,112},{112,128},... | collective-permute-start | bytes 5898248 | tf_op jit(solution)/shard_map/ppermute | solution.py:212
  96.5 1.9 %collective-permute-start.1 = (bf16[2,240,2048]{2,1,0:T(8,128)(2,1)S(1)}, bf16[2,240,2048]{2,1,0:T(8,128)(2,1)}, u32[]{:S(2)}, u32[]{:S(2)}) collective-permute-start(bf16[2,240,2048]{2,1,0:T(8,128)(2,1)S(1)} %copy-done.4), channel_id=1, source_target_pairs={{16,0},{32,16},{48,32},{64,48},{80,64},{96,80},{112,96},{128,112},... | collective-permute-start | bytes 5898248 | tf_op jit(solution)/shard_map/ppermute | solution.py:213
  98.4 18.4 %attend.1 = bf16[16,225,128]{2,1,0:T(8,128)(2,1)} custom-call(bf16[16,688,128]{2,1,0:T(8,128)(2,1)S(1)} %all_to_all.10.got_ref), custom_call_target="tpu_custom_call" | custom-call | flops 6635520000 | bytes 3686400 | tf_op jit(solution)/shard_map/attend/pallas_call | solution.py:108
  116.8 1.2 collective-permute-done.before_ref
  118.1 6.6 %collective-permute-done.1.after_ref = bf16[2,240,2048]{2,1,0:T(8,128)(2,1)} collective-permute-done((bf16[2,240,2048]{2,1,0:T(8,128)(2,1)S(1)}, bf16[2,240,2048]{2,1,0:T(8,128)(2,1)}, u32[]{:S(2)}, u32[]{:S(2)}) %collective-permute-start.1) | collective-permute-done | bytes 1966112 | tf_op jit(solution)/shard_map/ppermute | solution.py:213
  124.7 3.6 %all-to-all-start.1 = ((bf16[16,225,128]{2,1,0:T(8,128)(2,1)}), bf16[16,225,128]{2,1,0:T(8,128)(2,1)S(1)}, u32[]{:S(2)}, u32[]{:S(2)}) async-start(bf16[16,225,128]{2,1,0:T(8,128)(2,1)} %attend.1), calls=%async_computation.1 | async-start | bytes 1900544 | tf_op jit(solution)/shard_map/all_to_all | solution.py:217
  128.3 0.0 copy-done.3
  128.3 0.6 fusion
  130.9 0.6 add_convert_fusion.usable_ref
  131.5 0.0 copy-done
  131.5 0.6 constant_dynamic-slice_fusion.gate_ref
  132.1 0.0 copy-done.2
  132.1 6.3 %temporal.1.temporal_ref = f32[1,225,2048]{2,1,0:T(8,128)} custom-call(s32[3]{0:T(128)} %add_convert_fusion.usable_ref, bf16[1,225,2048]{2,1,0:T(8,128)(2,1)} %q_ref.3, bf16[1,225,2048]{2,1,0:T(8,128)(2,1)} %k_ref.3, bf16[1,225,2048]{2,1,0:T(8,128)(2,1)} %v_ref.3, bf16[2,240,2048]{2,1,0:T(8,128)(2,1)} %copy-done.2, ...), custom_call_target="tpu_custom_call" | custom-call | flops 5529600 | bytes 8294400 | tf_op jit(solution)/shard_map/temporal/pallas_call | solution.py:152
  138.5 15.5 %all-to-all-done.1.spatial_ref = bf16[16,225,128]{2,1,0:T(8,128)(2,1)S(1)} async-done(((bf16[16,225,128]{2,1,0:T(8,128)(2,1)}), bf16[16,225,128]{2,1,0:T(8,128)(2,1)S(1)}, u32[]{:S(2)}, u32[]{:S(2)}) %all-to-all-start.1) | async-done | bytes 921632 | tf_op jit(solution)/shard_map/all_to_all | solution.py:217
  154.0 0.9 copy-done.1
  154.9 4.3 %finish.1 = bf16[1,225,2048]{2,1,0:T(8,128)(2,1)} custom-call(s32[1]{0:T(128)} %bitcast.first_ref, bf16[16,225,128]{2,1,0:T(8,128)(2,1)} %copy-done.1, f32[1,225,2048]{2,1,0:T(8,128)} %temporal.1.temporal_ref, bf16[1,225,2048]{2,1,0:T(8,128)(2,1)} %residual_ref.1, f32[1,2048]{1,0:T(1,128)} %constant_dynamic-slice_fusion.gate_ref, bf16[225,2048]{1,0:T(8,128)(2,1)} %fresh_ref.1), custom_call_target="tpu_custom_call" | custom-call | flops 1843200 | bytes 5529600 | tf_op jit(solution)/shard_map/finish/pallas_call | solution.py:177
  159.3 1.9 %collective-permute-start.2 = (bf16[1,225,2048]{2,1,0:T(8,128)(2,1)}, bf16[1,225,2048]{2,1,0:T(8,128)(2,1)S(1)}, u32[]{:S(2)}, u32[]{:S(2)}) collective-permute-start(bf16[1,225,2048]{2,1,0:T(8,128)(2,1)} %finish.1), channel_id=1, source_target_pairs={{0,496},{16,0},{32,16},{48,32},{64,48},{80,64},{96,80},{112,96},{1... | collective-permute-start | bytes 2764808 | tf_op jit(solution)/shard_map/ppermute | solution.py:219
  161.2 15.5 %collective-permute-done.2 = bf16[1,225,2048]{2,1,0:T(8,128)(2,1)S(1)} collective-permute-done((bf16[1,225,2048]{2,1,0:T(8,128)(2,1)}, bf16[1,225,2048]{2,1,0:T(8,128)(2,1)S(1)}, u32[]{:S(2)}, u32[]{:S(2)}) %collective-permute-start.2) | collective-permute-done | bytes 921632 | tf_op jit(solution)/shard_map/ppermute | solution.py:219
  176.7 0.9 copy.11
  (3 shorter events, 0.0 us)
Async XLA Ops:
  0.0 131.5 %copy-start = (f32[64,2048]{1,0:T(8,128)S(1)}, f32[64,2048]{1,0:T(8,128)}, u32[]{:S(2)}) copy-start(f32[64,2048]{1,0:T(8,128)} %param.14) | copy-start | bytes 1572868
  4.9 78.9 %copy-start.4 = (bf16[2,240,2048]{2,1,0:T(8,128)(2,1)S(1)}, bf16[2,240,2048]{2,1,0:T(8,128)(2,1)}, u32[]{:S(2)}) copy-start(bf16[2,240,2048]{2,1,0:T(8,128)(2,1)} %get-tuple-element.15) | copy-start | bytes 5898244
  83.8 44.6 %copy-start.3 = (s32[1,2]{1,0:T(1,128)S(1)}, s32[1,2]{1,0:T(1,128)}, u32[]{:S(2)}) copy-start(s32[1,2]{1,0:T(1,128)} %param.13) | copy-start | bytes 28
  83.8 34.3 %collective-permute-start = (bf16[2,240,2048]{2,1,0:T(8,128)(2,1)S(1)}, bf16[2,240,2048]{2,1,0:T(8,128)(2,1)S(1)}, u32[]{:S(2)}, u32[]{:S(2)}) collective-permute-start(bf16[2,240,2048]{2,1,0:T(8,128)(2,1)S(1)} %copy-done.4), channel_id=1, source_target_pairs={{0,16},{16,32},{32,48},{48,64},{64,80},{80,96},{96,112},{112,128},... | collective-permute-start | bytes 5898248 | tf_op jit(solution)/shard_map/ppermute | solution.py:212
  96.5 28.2 %collective-permute-start.1 = (bf16[2,240,2048]{2,1,0:T(8,128)(2,1)S(1)}, bf16[2,240,2048]{2,1,0:T(8,128)(2,1)}, u32[]{:S(2)}, u32[]{:S(2)}) collective-permute-start(bf16[2,240,2048]{2,1,0:T(8,128)(2,1)S(1)} %copy-done.4), channel_id=1, source_target_pairs={{16,0},{32,16},{48,32},{64,48},{80,64},{96,80},{112,96},{128,112},... | collective-permute-start | bytes 5898248 | tf_op jit(solution)/shard_map/ppermute | solution.py:213
  118.1 14.1 %copy-start.2 = (bf16[2,240,2048]{2,1,0:T(8,128)(2,1)}, bf16[2,240,2048]{2,1,0:T(8,128)(2,1)S(1)}, u32[]{:S(2)}) copy-start(bf16[2,240,2048]{2,1,0:T(8,128)(2,1)S(1)} %collective-permute-done.before_ref) | copy-start | bytes 5898244
  124.7 29.3 %all-to-all-start.1 = ((bf16[16,225,128]{2,1,0:T(8,128)(2,1)}), bf16[16,225,128]{2,1,0:T(8,128)(2,1)S(1)}, u32[]{:S(2)}, u32[]{:S(2)}) async-start(bf16[16,225,128]{2,1,0:T(8,128)(2,1)} %attend.1), calls=%async_computation.1 | async-start | bytes 1900544 | tf_op jit(solution)/shard_map/all_to_all | solution.py:217
  154.0 0.9 copy-start.1
  159.3 17.4 %collective-permute-start.2 = (bf16[1,225,2048]{2,1,0:T(8,128)(2,1)}, bf16[1,225,2048]{2,1,0:T(8,128)(2,1)S(1)}, u32[]{:S(2)}, u32[]{:S(2)}) collective-permute-start(bf16[1,225,2048]{2,1,0:T(8,128)(2,1)} %finish.1), channel_id=1, source_target_pairs={{0,496},{16,0},{32,16},{48,32},{64,48},{80,64},{96,80},{112,96},{1... | collective-permute-start | bytes 2764808 | tf_op jit(solution)/shard_map/ppermute | solution.py:219

commit v3 on v2

--- a/solution.py
+++ b/solution.py
@@ -14,6 +14,7 @@
 MASKED = -1e30
 MIB = 1024 * 1024
 STEP_HEADS = 4
+TAIL = 8
 QUERY_BLOCK = 720
 KEY_BLOCK = 720
 
@@ -26,9 +27,9 @@
     for part, ref in enumerate((k_ref, v_ref)):
         own_ref[part, main:, :] = jnp.zeros_like(own_ref[part, main:, :])
         own_ref[part, : main + 1, :] = ref[0]
-    row = lax.broadcasted_iota(jnp.int32, (16, HEAD_DIM), 0)
+    row = lax.broadcasted_iota(jnp.int32, (TAIL, HEAD_DIM), 0)
     for head in range(STEP_HEADS):
-        tail = jnp.zeros((16, HEAD_DIM), jnp.float32)
+        tail = jnp.zeros((TAIL, HEAD_DIM), jnp.float32)
         for part, ref in enumerate((q_ref, k_ref, v_ref)):
             out_ref[head, part * main : (part + 1) * main, :] = ref[0, :main, columns(head)]
             last = ref[0, main : main + 1, columns(head)].astype(jnp.float32)
@@ -40,7 +41,7 @@
     _, rows, channels = queries.shape
     heads = channels // HEAD_DIM
     main = rows - 1
-    total = 3 * main + 16
+    total = 3 * main + TAIL
     spec = pl.BlockSpec((1, rows, STEP_HEADS * HEAD_DIM), lambda h: (0, 0, h))
     return pl.pallas_call(
         functools.partial(pack_kernel, main=main),
@@ -48,11 +49,11 @@
         in_specs=[spec] * 3,
         out_specs=[
             pl.BlockSpec((STEP_HEADS, total, HEAD_DIM), lambda h: (h, 0, 0)),
-            pl.BlockSpec((2, main + 16, STEP_HEADS * HEAD_DIM), lambda h: (0, 0, h)),
+            pl.BlockSpec((2, main + 8, STEP_HEADS * HEAD_DIM), lambda h: (0, 0, h)),
         ],
         out_shape=[
             jax.ShapeDtypeStruct((heads, total, HEAD_DIM), jnp.bfloat16),
-            jax.ShapeDtypeStruct((2, main + 16, channels), jnp.bfloat16),
+            jax.ShapeDtypeStruct((2, main + 8, channels), jnp.bfloat16),
         ],
         cost_estimate=pl.CostEstimate(flops=0, bytes_accessed=8 * queries.size * 2, transcendentals=0),
         name="pack",
@@ -124,13 +125,13 @@
     )(got)
 
 
-def temporal_kernel(usable_ref, q_ref, k_ref, v_ref, before_ref, after_ref, out_ref):
+def temporal_kernel(usable_ref, q_ref, k_ref, v_ref, near_k_ref, near_v_ref, far_ref, out_ref):
     rows = q_ref.shape[1]
     for head in range(STEP_HEADS):
         at = columns(head)
         q = q_ref[0, :, at].astype(jnp.float32)
-        keys = (before_ref[0, :rows, at], k_ref[0, :, at], after_ref[0, :rows, at])
-        values = (before_ref[1, :rows, at], v_ref[0, :, at], after_ref[1, :rows, at])
+        keys = (k_ref[0, :, at], near_k_ref[0, :, at], far_ref[0, :rows, at])
+        values = (v_ref[0, :, at], near_v_ref[0, :, at], far_ref[1, :rows, at])
         scores = []
         for j in range(3):
             score = jnp.sum(q * keys[j].astype(jnp.float32), axis=1, keepdims=True) * SCALE
@@ -144,49 +145,38 @@
         out_ref[0, :, at] = summed / total
 
 
-def temporal_attend(usable, queries, keys, values, before, after):
+def temporal_attend(usable, queries, keys, values, near_keys, near_values, far):
     _, rows, channels = queries.shape
     width = STEP_HEADS * HEAD_DIM
     spec = pl.BlockSpec((1, rows, width), lambda h: (0, 0, h))
-    pair = pl.BlockSpec((2, before.shape[1], width), lambda h: (0, 0, h))
+    pair = pl.BlockSpec((2, far.shape[1], width), lambda h: (0, 0, h))
     return pl.pallas_call(
         temporal_kernel,
         grid=(channels // width,),
-        in_specs=[pl.BlockSpec(memory_space=pltpu.SMEM), spec, spec, spec, pair, pair],
+        in_specs=[pl.BlockSpec(memory_space=pltpu.SMEM)] + [spec] * 5 + [pair],
         out_specs=spec,
         out_shape=jax.ShapeDtypeStruct(queries.shape, jnp.float32),
         cost_estimate=pl.CostEstimate(flops=12 * queries.size, bytes_accessed=18 * queries.size, transcendentals=0),
         name="temporal",
-    )(usable, queries, keys, values, before, after)
+    )(usable, queries, keys, values, near_keys, near_values, far)
 
 
 def finish_kernel(first_ref, spatial_ref, temporal_ref, residual_ref, gate_ref, fresh_ref, out_ref):
     is_first = first_ref[0] > 0
-    for head in range(STEP_HEADS):
+    for head in range(spatial_ref.shape[0]):
         at = columns(head)
         mixed = (spatial_ref[head].astype(jnp.float32) + temporal_ref[0, :, at]).astype(jnp.bfloat16)
         updated = residual_ref[0, :, at].astype(jnp.float32) + gate_ref[:, at] * mixed.astype(jnp.float32)
-        fresh = fresh_ref[:, at].astype(jnp.float32)
-        out_ref[0, :, at] = jnp.where(is_first, fresh, updated).astype(jnp.bfloat16)
+        out_ref[0, :, at] = jnp.where(is_first, fresh_ref[:, at].astype(jnp.float32), updated).astype(jnp.bfloat16)
 
 
 def finish(is_first, spatial, temporal, residual, gate_row, fresh):
-    heads, rows, _ = spatial.shape
-    width = STEP_HEADS * HEAD_DIM
-    by_head = pl.BlockSpec((1, rows, width), lambda h: (0, 0, h))
     return pl.pallas_call(
         finish_kernel,
-        grid=(heads // STEP_HEADS,),
-        in_specs=[
-            pl.BlockSpec(memory_space=pltpu.SMEM),
-            pl.BlockSpec((STEP_HEADS, rows, HEAD_DIM), lambda h: (h, 0, 0)),
-            by_head,
-            by_head,
-            pl.BlockSpec((1, width), lambda h: (0, h)),
-            pl.BlockSpec((rows, width), lambda h: (0, h)),
-        ],
-        out_specs=by_head,
+        in_specs=[pl.BlockSpec(memory_space=pltpu.SMEM)] + [pl.BlockSpec(memory_space=pltpu.VMEM)] * 5,
+        out_specs=pl.BlockSpec(memory_space=pltpu.VMEM),
         out_shape=jax.ShapeDtypeStruct(residual.shape, jnp.bfloat16),
+        compiler_params=pltpu.CompilerParams(vmem_limit_bytes=16 * MIB),
         cost_estimate=pl.CostEstimate(flops=4 * residual.size, bytes_accessed=12 * residual.size, transcendentals=0),
         name="finish",
     )(is_first, spatial, temporal, residual, gate_row, fresh)
@@ -196,24 +186,27 @@
     rows = head_queries.shape[1]
     frame = lax.axis_index("queue")
     frames = lax.axis_size("queue")
-    up = [(i, i + 1) for i in range(frames - 1)]
-    down = [(j, i) for i, j in up]
+    near_pairs = [(i, i ^ 1) for i in range(frames)]
+    far_pairs = [(i, j) for i, j in ((i, ((i + 1) ^ 1) - 1) for i in range(frames)) if 0 <= j < frames]
 
     sent, own = pack(head_queries, head_keys, head_values)
     got = lax.all_to_all(sent, "space", split_axis=0, concat_axis=0, tiled=True)
-
+    got, own, window, levels = lax.optimization_barrier((got, own, window, levels))
+
+    far = lax.ppermute(own, "queue", far_pairs)
     before = (window[0, 0] >= 1) & (frame >= 1)
     after = (window[0, 1] >= 1) & (frame <= frames - 2)
-    usable = jnp.stack([before, jnp.bool_(True), after]).astype(jnp.int32)
+    odd = frame % 2 == 1
+    near_usable, far_usable = jnp.where(odd, before, after), jnp.where(odd, after, before)
+    usable = jnp.stack([jnp.bool_(True), near_usable, far_usable]).astype(jnp.int32)
+    is_first = (frame == 0).astype(jnp.int32)[None]
     gate_row = lax.dynamic_slice_in_dim(level_gate, levels[0], 1, axis=0)
-    is_first = (frame == 0).astype(jnp.int32)[None]
-
-    got, own = lax.optimization_barrier((got, own))
-    from_before = lax.ppermute(own, "queue", up)
-    from_after = lax.ppermute(own, "queue", down)
     back = attend(got, rows)
-    back, from_before, from_after = lax.optimization_barrier((back, from_before, from_after))
-    temporal = temporal_attend(usable, head_queries, head_keys, head_values, from_before, from_after)
+    back, far, head_keys, head_values = lax.optimization_barrier((back, far, head_keys, head_values))
+
+    near_keys = lax.ppermute(head_keys, "queue", near_pairs)
+    near_values = lax.ppermute(head_values, "queue", near_pairs)
+    temporal = temporal_attend(usable, head_queries, head_keys, head_values, near_keys, near_values, far)
     spatial = lax.all_to_all(back, "space", split_axis=0, concat_axis=0, tiled=True)
     updated = finish(is_first, spatial, temporal, residual, gate_row, fresh_frame)
     return lax.ppermute(updated, "queue", [(i, (i - 1) % frames) for i in range(frames)])

time: 178 us -> 172 us (0.966)
  waiting for transfers between devices: 38.9 us -> 32.3 us
  starting transfers between devices: 20.2 us -> 25 us
  Pallas kernels: 33.9 us -> 30.4 us
    ppermute x2 -> x3, waiting for transfers between devices: 7.85 us -> 3.33 us  [the longest x1 3.32 us: on_device(): far = lax.ppermute(own, 'queue', far_pairs)]
    pallas_call x1, Pallas kernels: 4.33 us -> 0.61 us  [finish(): pl.pallas_call(finish_kernel, in_specs=[pl.BlockSpec(memory_space=pltpu.S...]
    ppermute x2 -> x3, starting transfers between devices: 14.7 us -> 17.5 us  [the longest x1 13.2 us: on_device(): far = lax.ppermute(own, 'queue', far_pairs)]
  transfers between devices with their start and end apart: 4 -> 5, of which waited for: 4 -> 3; matrix products, arithmetic and copies ran while one was open for 1% -> 1% of each run, Pallas kernels for 14% -> 15%
where the time goes in v3:
time: 172 us; the launch traced here: 171 us
  blocking collectives  77.8 us (45%)
  waiting for transfers between devices  32.3 us (19%)
  Pallas kernels  30.4 us (18%)
  starting transfers between devices  25 us (15%)
  local copies, waits for them, and re-layouts  3.08 us (2%)
  between operations  2.01 us (1%)
    all_to_all x1, blocking collectives, on_device(): got = lax.all_to_all(sent, 'space', split_axis=0, concat_axis=0, tiled=True)  77.8 us
    pallas_call x1, Pallas kernels, attend(): pl.pallas_call(functools.partial(attend_kernel, sources=sources, main=mai...  18.4 us
    ppermute x1, waiting for transfers between devices, on_device(): lax.ppermute(updated, 'queue', [(i, (i - 1) % frames) for i in range(fram...  14.9 us
    all_to_all x1, waiting for transfers between devices, on_device(): lax.all_to_all(back, 'space', split_axis=0, concat_axis=0, tiled=True)  14 us
    ppermute x1, starting transfers between devices, on_device(): far = lax.ppermute(own, 'queue', far_pairs)  13.2 us
    pallas_call x1, Pallas kernels, temporal_attend(): pl.pallas_call(temporal_kernel, grid=(channels // width,), in_specs=[pl.B...  6.59 us
    all_to_all x1, starting transfers between devices, on_device(): lax.all_to_all(back, 'space', split_axis=0, concat_axis=0, tiled=True)  5.18 us
    pallas_call x1, Pallas kernels, pack(): pl.pallas_call(functools.partial(pack_kernel, main=main), grid=(heads //...  4.85 us
  transfers between devices with their start and end apart: 5, of which 3 were waited for; matrix products, arithmetic and copies ran while one was open for 1% of the time, Pallas kernels for 15%

profile of v3, /device:TPU:7, one launch (start us, length us, event | category | flops | bytes accessed | tf_op | source)
XLA Modules:
  0.0 171.2 jit_solution(5916077006511935936)
XLA Ops:
  0.0 0.0 copy-start
  0.0 4.9 %pack.1 = (bf16[16,680,128]{2,1,0:T(8,128)(2,1)}, bf16[2,232,2048]{2,1,0:T(8,128)(2,1)}) custom-call(bf16[1,225,2048]{2,1,0:T(8,128)(2,1)} %q_ref.3, bf16[1,225,2048]{2,1,0:T(8,128)(2,1)} %k_ref.2, bf16[1,225,2048]{2,1,0:T(8,128)(2,1)} %v_ref.2), custom_call_target="tpu_custom_call" | custom-call | bytes 7372800 | tf_op jit(solution)/shard_map/pack/pallas_call | solution.py:46
  4.9 77.8 %all_to_all.10.got_ref = bf16[16,680,128]{2,1,0:T(8,128)(2,1)S(1)} all-to-all(bf16[16,680,128]{2,1,0:T(8,128)(2,1)} %get-tuple-element.15), channel_id=1, replica_groups=mesh['queue'=32,'space'=16] {'space'}, dimensions={0} | all-to-all | bytes 5570560 | tf_op jit(solution)/shard_map/all_to_all | solution.py:193
  82.7 0.0 copy-done.5
  82.7 13.2 %collective-permute-start = (bf16[2,232,2048]{2,1,0:T(8,128)(2,1)S(1)}, bf16[2,232,2048]{2,1,0:T(8,128)(2,1)}, u32[]{:S(2)}, u32[]{:S(2)}) collective-permute-start(bf16[2,232,2048]{2,1,0:T(8,128)(2,1)S(1)} %copy-done.5), channel_id=1, source_target_pairs={{16,32},{32,16},{48,64},{64,48},{80,96},{96,80},{112,128},{128,112... | collective-permute-start | bytes 5701640 | tf_op jit(solution)/shard_map/ppermute | solution.py:196
  95.9 18.4 %attend.1 = bf16[16,225,128]{2,1,0:T(8,128)(2,1)} custom-call(bf16[16,680,128]{2,1,0:T(8,128)(2,1)S(1)} %all_to_all.10.got_ref), custom_call_target="tpu_custom_call" | custom-call | flops 6635520000 | bytes 3686400 | tf_op jit(solution)/shard_map/attend/pallas_call | solution.py:109
  114.2 3.3 %collective-permute-done.far_ref = bf16[2,232,2048]{2,1,0:T(8,128)(2,1)} collective-permute-done((bf16[2,232,2048]{2,1,0:T(8,128)(2,1)S(1)}, bf16[2,232,2048]{2,1,0:T(8,128)(2,1)}, u32[]{:S(2)}, u32[]{:S(2)}) %collective-permute-start) | collective-permute-done | bytes 1900576 | tf_op jit(solution)/shard_map/ppermute | solution.py:196
  117.6 5.2 %all-to-all-start.1 = ((bf16[16,225,128]{2,1,0:T(8,128)(2,1)}), bf16[16,225,128]{2,1,0:T(8,128)(2,1)S(1)}, u32[]{:S(2)}, u32[]{:S(2)}) async-start(bf16[16,225,128]{2,1,0:T(8,128)(2,1)} %attend.1), calls=%async_computation.1 | async-start | bytes 1900544 | tf_op jit(solution)/shard_map/all_to_all | solution.py:210
  122.7 1.9 %collective-permute-start.1 = (bf16[1,225,2048]{2,1,0:T(8,128)(2,1)}, bf16[1,225,2048]{2,1,0:T(8,128)(2,1)}, u32[]{:S(2)}, u32[]{:S(2)}) collective-permute-start(bf16[1,225,2048]{2,1,0:T(8,128)(2,1)} %k_ref.2), channel_id=1, source_target_pairs={{0,16},{16,0},{32,48},{48,32},{64,80},{80,64},{96,112},{112,96},{1... | collective-permute-start | bytes 2764808 | tf_op jit(solution)/shard_map/ppermute | solution.py:207
  124.7 2.4 %collective-permute-start.2 = (bf16[1,225,2048]{2,1,0:T(8,128)(2,1)}, bf16[1,225,2048]{2,1,0:T(8,128)(2,1)}, u32[]{:S(2)}, u32[]{:S(2)}) collective-permute-start(bf16[1,225,2048]{2,1,0:T(8,128)(2,1)} %v_ref.2), channel_id=1, source_target_pairs={{0,16},{16,0},{32,48},{48,32},{64,80},{80,64},{96,112},{112,96},{1... | collective-permute-start | bytes 2764808 | tf_op jit(solution)/shard_map/ppermute | solution.py:208
  127.8 0.0 copy-done
  127.8 0.0 copy-done.4
  127.8 0.6 fusion
  129.7 0.6 add_convert_fusion.usable_ref
  130.3 0.0 collective-permute-done.1.near_k_ref
  130.3 0.0 collective-permute-done.2.near_v_ref
  130.3 6.6 %temporal.1.temporal_ref = f32[1,225,2048]{2,1,0:T(8,128)} custom-call(s32[3]{0:T(128)} %add_convert_fusion.usable_ref, bf16[1,225,2048]{2,1,0:T(8,128)(2,1)} %q_ref.3, bf16[1,225,2048]{2,1,0:T(8,128)(2,1)} %k_ref.2, bf16[1,225,2048]{2,1,0:T(8,128)(2,1)} %v_ref.2, bf16[1,225,2048]{2,1,0:T(8,128)(2,1)} %collective-permute-done.1.near_k_ref, ...), custom_call_target="tpu_custom_call" | custom-call | flops 5529600 | bytes 8294400 | tf_op jit(solution)/shard_map/temporal/pallas_call | solution.py:153
  136.9 14.0 %all-to-all-done.1.spatial_ref = bf16[16,225,128]{2,1,0:T(8,128)(2,1)S(1)} async-done(((bf16[16,225,128]{2,1,0:T(8,128)(2,1)}), bf16[16,225,128]{2,1,0:T(8,128)(2,1)S(1)}, u32[]{:S(2)}, u32[]{:S(2)}) %all-to-all-start.1) | async-done | bytes 921632 | tf_op jit(solution)/shard_map/all_to_all | solution.py:210
  150.9 0.0 copy-done.2
  150.9 1.5 copy-done.1
  152.4 0.6 finish.1
  153.1 2.3 %collective-permute-start.3 = (bf16[1,225,2048]{2,1,0:T(8,128)(2,1)S(1)}, bf16[1,225,2048]{2,1,0:T(8,128)(2,1)S(1)}, u32[]{:S(2)}, u32[]{:S(2)}) collective-permute-start(bf16[1,225,2048]{2,1,0:T(8,128)(2,1)S(1)} %finish.1), channel_id=1, source_target_pairs={{0,496},{16,0},{32,16},{48,32},{64,48},{80,64},{96,80},{112,96},{1... | collective-permute-start | bytes 2764808 | tf_op jit(solution)/shard_map/ppermute | solution.py:212
  155.3 14.9 %collective-permute-done.3 = bf16[1,225,2048]{2,1,0:T(8,128)(2,1)S(1)} collective-permute-done((bf16[1,225,2048]{2,1,0:T(8,128)(2,1)S(1)}, bf16[1,225,2048]{2,1,0:T(8,128)(2,1)S(1)}, u32[]{:S(2)}, u32[]{:S(2)}) %collective-permute-start.3) | collective-permute-done | bytes 921632 | tf_op jit(solution)/shard_map/ppermute | solution.py:212
  170.2 0.9 copy.11
  (7 shorter events, 0.0 us)
Async XLA Ops:
  0.0 127.8 %copy-start = (f32[64,2048]{1,0:T(8,128)S(1)}, f32[64,2048]{1,0:T(8,128)}, u32[]{:S(2)}) copy-start(f32[64,2048]{1,0:T(8,128)} %param.14) | copy-start | bytes 1572868
  4.9 77.8 %copy-start.5 = (bf16[2,232,2048]{2,1,0:T(8,128)(2,1)S(1)}, bf16[2,232,2048]{2,1,0:T(8,128)(2,1)}, u32[]{:S(2)}) copy-start(bf16[2,232,2048]{2,1,0:T(8,128)(2,1)} %get-tuple-element.18) | copy-start | bytes 5701636
  82.7 34.9 %collective-permute-start = (bf16[2,232,2048]{2,1,0:T(8,128)(2,1)S(1)}, bf16[2,232,2048]{2,1,0:T(8,128)(2,1)}, u32[]{:S(2)}, u32[]{:S(2)}) collective-permute-start(bf16[2,232,2048]{2,1,0:T(8,128)(2,1)S(1)} %copy-done.5), channel_id=1, source_target_pairs={{16,32},{32,16},{48,64},{64,48},{80,96},{96,80},{112,128},{128,112... | collective-permute-start | bytes 5701640 | tf_op jit(solution)/shard_map/ppermute | solution.py:196
  114.2 13.6 %copy-start.4 = (s32[1,2]{1,0:T(1,128)S(1)}, s32[1,2]{1,0:T(1,128)}, u32[]{:S(2)}) copy-start(s32[1,2]{1,0:T(1,128)} %param.13) | copy-start | bytes 28
  117.6 33.4 %all-to-all-start.1 = ((bf16[16,225,128]{2,1,0:T(8,128)(2,1)}), bf16[16,225,128]{2,1,0:T(8,128)(2,1)S(1)}, u32[]{:S(2)}, u32[]{:S(2)}) async-start(bf16[16,225,128]{2,1,0:T(8,128)(2,1)} %attend.1), calls=%async_computation.1 | async-start | bytes 1900544 | tf_op jit(solution)/shard_map/all_to_all | solution.py:210
  122.7 7.5 %collective-permute-start.1 = (bf16[1,225,2048]{2,1,0:T(8,128)(2,1)}, bf16[1,225,2048]{2,1,0:T(8,128)(2,1)}, u32[]{:S(2)}, u32[]{:S(2)}) collective-permute-start(bf16[1,225,2048]{2,1,0:T(8,128)(2,1)} %k_ref.2), channel_id=1, source_target_pairs={{0,16},{16,0},{32,48},{48,32},{64,80},{80,64},{96,112},{112,96},{1... | collective-permute-start | bytes 2764808 | tf_op jit(solution)/shard_map/ppermute | solution.py:207
  124.7 5.6 %collective-permute-start.2 = (bf16[1,225,2048]{2,1,0:T(8,128)(2,1)}, bf16[1,225,2048]{2,1,0:T(8,128)(2,1)}, u32[]{:S(2)}, u32[]{:S(2)}) collective-permute-start(bf16[1,225,2048]{2,1,0:T(8,128)(2,1)} %v_ref.2), channel_id=1, source_target_pairs={{0,16},{16,0},{32,48},{48,32},{64,80},{80,64},{96,112},{112,96},{1... | collective-permute-start | bytes 2764808 | tf_op jit(solution)/shard_map/ppermute | solution.py:208
  130.3 20.6 %copy-start.2 = (bf16[1,225,2048]{2,1,0:T(8,128)(2,1)S(1)}, bf16[1,225,2048]{2,1,0:T(8,128)(2,1)}, u32[]{:S(2)}) copy-start(bf16[1,225,2048]{2,1,0:T(8,128)(2,1)} %residual_ref.1) | copy-start | bytes 2764804
  130.3 20.6 %copy-start.3 = (bf16[225,2048]{1,0:T(8,128)(2,1)S(1)}, bf16[225,2048]{1,0:T(8,128)(2,1)}, u32[]{:S(2)}) copy-start(bf16[225,2048]{1,0:T(8,128)(2,1)} %fresh_ref.1) | copy-start | bytes 2764804
  150.9 1.5 copy-start.1
  153.1 17.2 %collective-permute-start.3 = (bf16[1,225,2048]{2,1,0:T(8,128)(2,1)S(1)}, bf16[1,225,2048]{2,1,0:T(8,128)(2,1)S(1)}, u32[]{:S(2)}, u32[]{:S(2)}) collective-permute-start(bf16[1,225,2048]{2,1,0:T(8,128)(2,1)S(1)} %finish.1), channel_id=1, source_target_pairs={{0,496},{16,0},{32,16},{48,32},{64,48},{80,64},{96,80},{112,96},{1... | collective-permute-start | bytes 2764808 | tf_op jit(solution)/shard_map/ppermute | solution.py:212

commit v4 on v3

--- a/solution.py
+++ b/solution.py
@@ -15,6 +15,7 @@
 MIB = 1024 * 1024
 STEP_HEADS = 4
 TAIL = 8
+TEMPORAL_FLOPS = 5 * 10**9
 QUERY_BLOCK = 720
 KEY_BLOCK = 720
 
@@ -156,7 +157,7 @@
         in_specs=[pl.BlockSpec(memory_space=pltpu.SMEM)] + [spec] * 5 + [pair],
         out_specs=spec,
         out_shape=jax.ShapeDtypeStruct(queries.shape, jnp.float32),
-        cost_estimate=pl.CostEstimate(flops=12 * queries.size, bytes_accessed=18 * queries.size, transcendentals=0),
+        cost_estimate=pl.CostEstimate(flops=TEMPORAL_FLOPS, bytes_accessed=18 * queries.size, transcendentals=0),
         name="temporal",
     )(usable, queries, keys, values, near_keys, near_values, far)
 
@@ -202,7 +203,7 @@
     is_first = (frame == 0).astype(jnp.int32)[None]
     gate_row = lax.dynamic_slice_in_dim(level_gate, levels[0], 1, axis=0)
     back = attend(got, rows)
-    back, far, head_keys, head_values = lax.optimization_barrier((back, far, head_keys, head_values))
+    far, head_keys, head_values, _ = lax.optimization_barrier((far, head_keys, head_values, back))
 
     near_keys = lax.ppermute(head_keys, "queue", near_pairs)
     near_values = lax.ppermute(head_values, "queue", near_pairs)

time: 172 us -> 166 us (0.965)
  waiting for transfers between devices: 32.3 us -> 28.6 us
    ppermute x1, waiting for transfers between devices: 3.32 us -> 0.01 us  [on_device(): far = lax.ppermute(own, 'queue', far_pairs)]
  transfers between devices with their start and end apart: 5 -> 5, of which waited for: 3 -> 2; matrix products, arithmetic and copies ran while one was open for 1% -> 1% of each run, Pallas kernels for 15% -> 15%
where the time goes in v4:
time: 166 us
  blocking collectives  77.7 us (47%)
  Pallas kernels  30.4 us (18%)
  waiting for transfers between devices  28.6 us (17%)
  starting transfers between devices  23.5 us (14%)
  local copies, waits for them, and re-layouts  3.08 us (2%)
  between operations  2.03 us (1%)
    all_to_all x1, blocking collectives, on_device(): got = lax.all_to_all(sent, 'space', split_axis=0, concat_axis=0, tiled=True)  77.7 us
    pallas_call x1, Pallas kernels, attend(): pl.pallas_call(functools.partial(attend_kernel, sources=sources, main=mai...  18.4 us
    ppermute x1, waiting for transfers between devices, on_device(): lax.ppermute(updated, 'queue', [(i, (i - 1) % frames) for i in range(fram...  15 us
    all_to_all x1, waiting for transfers between devices, on_device(): lax.all_to_all(back, 'space', split_axis=0, concat_axis=0, tiled=True)  13.6 us
    ppermute x1, starting transfers between devices, on_device(): far = lax.ppermute(own, 'queue', far_pairs)  13.2 us
    pallas_call x1, Pallas kernels, temporal_attend(): pl.pallas_call(temporal_kernel, grid=(channels // width,), in_specs=[pl.B...  6.59 us
    pallas_call x1, Pallas kernels, pack(): pl.pallas_call(functools.partial(pack_kernel, main=main), grid=(heads //...  4.85 us
    all_to_all x1, starting transfers between devices, on_device(): lax.all_to_all(back, 'space', split_axis=0, concat_axis=0, tiled=True)  3.77 us
  transfers between devices with their start and end apart: 5, of which 2 were waited for; matrix products, arithmetic and copies ran while one was open for 1% of the time, Pallas kernels for 15%

profile of v4, /device:TPU:7, one launch (start us, length us, event | category | flops | bytes accessed | tf_op | source)
XLA Modules:
  0.0 165.9 jit_solution(5438042377496156427)
XLA Ops:
  0.0 0.0 copy-start
  0.0 4.9 %pack.1 = (bf16[16,680,128]{2,1,0:T(8,128)(2,1)}, bf16[2,232,2048]{2,1,0:T(8,128)(2,1)}) custom-call(bf16[1,225,2048]{2,1,0:T(8,128)(2,1)} %q_ref.3, bf16[1,225,2048]{2,1,0:T(8,128)(2,1)} %k_ref.2, bf16[1,225,2048]{2,1,0:T(8,128)(2,1)} %v_ref.2), custom_call_target="tpu_custom_call" | custom-call | bytes 7372800 | tf_op jit(solution)/shard_map/pack/pallas_call | solution.py:47
  4.9 77.7 %all_to_all.10.got_ref = bf16[16,680,128]{2,1,0:T(8,128)(2,1)S(1)} all-to-all(bf16[16,680,128]{2,1,0:T(8,128)(2,1)} %get-tuple-element.14), channel_id=1, replica_groups=mesh['queue'=32,'space'=16] {'space'}, dimensions={0} | all-to-all | bytes 5570560 | tf_op jit(solution)/shard_map/all_to_all | solution.py:194
  82.5 13.2 %collective-permute-start = (bf16[2,232,2048]{2,1,0:T(8,128)(2,1)}, bf16[2,232,2048]{2,1,0:T(8,128)(2,1)S(1)}, u32[]{:S(2)}, u32[]{:S(2)}) collective-permute-start(bf16[2,232,2048]{2,1,0:T(8,128)(2,1)} %get-tuple-element.18), channel_id=1, source_target_pairs={{16,32},{32,16},{48,64},{64,48},{80,96},{96,80},{112,128},{128,112... | collective-permute-start | bytes 5701640 | tf_op jit(solution)/shard_map/ppermute | solution.py:197
  95.7 18.4 %attend.1 = bf16[16,225,128]{2,1,0:T(8,128)(2,1)} custom-call(bf16[16,680,128]{2,1,0:T(8,128)(2,1)S(1)} %all_to_all.10.got_ref), custom_call_target="tpu_custom_call" | custom-call | flops 6635520000 | bytes 3686400 | tf_op jit(solution)/shard_map/attend/pallas_call | solution.py:110
  114.1 3.8 %all-to-all-start.1 = ((bf16[16,225,128]{2,1,0:T(8,128)(2,1)}), bf16[16,225,128]{2,1,0:T(8,128)(2,1)S(1)}, u32[]{:S(2)}, u32[]{:S(2)}) async-start(bf16[16,225,128]{2,1,0:T(8,128)(2,1)} %attend.1), calls=%async_computation.1 | async-start | bytes 1900544 | tf_op jit(solution)/shard_map/all_to_all | solution.py:211
  117.9 0.0 collective-permute-done.far_ref
  117.9 0.0 copy-start.5
  117.9 1.9 %collective-permute-start.1 = (bf16[1,225,2048]{2,1,0:T(8,128)(2,1)}, bf16[1,225,2048]{2,1,0:T(8,128)(2,1)}, u32[]{:S(2)}, u32[]{:S(2)}) collective-permute-start(bf16[1,225,2048]{2,1,0:T(8,128)(2,1)} %k_ref.2), channel_id=1, source_target_pairs={{0,16},{16,0},{32,48},{48,32},{64,80},{80,64},{96,112},{112,96},{1... | collective-permute-start | bytes 2764808 | tf_op jit(solution)/shard_map/ppermute | solution.py:208
  119.8 2.4 %collective-permute-start.2 = (bf16[1,225,2048]{2,1,0:T(8,128)(2,1)}, bf16[1,225,2048]{2,1,0:T(8,128)(2,1)}, u32[]{:S(2)}, u32[]{:S(2)}) collective-permute-start(bf16[1,225,2048]{2,1,0:T(8,128)(2,1)} %v_ref.2), channel_id=1, source_target_pairs={{0,16},{16,0},{32,48},{48,32},{64,80},{80,64},{96,112},{112,96},{1... | collective-permute-start | bytes 2764808 | tf_op jit(solution)/shard_map/ppermute | solution.py:209
  122.9 0.0 copy-done.5
  123.0 0.0 copy-done.4
  123.0 0.6 fusion
  124.8 0.6 add_convert_fusion.usable_ref
  125.4 0.0 collective-permute-done.1.near_k_ref
  125.4 0.0 collective-permute-done.2.near_v_ref
  125.4 6.6 %temporal.1.temporal_ref = f32[1,225,2048]{2,1,0:T(8,128)} custom-call(s32[3]{0:T(128)} %add_convert_fusion.usable_ref, bf16[1,225,2048]{2,1,0:T(8,128)(2,1)} %q_ref.3, bf16[1,225,2048]{2,1,0:T(8,128)(2,1)} %k_ref.2, bf16[1,225,2048]{2,1,0:T(8,128)(2,1)} %v_ref.2, bf16[1,225,2048]{2,1,0:T(8,128)(2,1)} %collective-permute-done.1.near_k_ref, ...), custom_call_target="tpu_custom_call" | custom-call | flops 5000000000 | bytes 8294400 | tf_op jit(solution)/shard_map/temporal/pallas_call | solution.py:154
  132.0 13.6 %all-to-all-done.1.spatial_ref = bf16[16,225,128]{2,1,0:T(8,128)(2,1)S(1)} async-done(((bf16[16,225,128]{2,1,0:T(8,128)(2,1)}), bf16[16,225,128]{2,1,0:T(8,128)(2,1)S(1)}, u32[]{:S(2)}, u32[]{:S(2)}) %all-to-all-start.1) | async-done | bytes 921632 | tf_op jit(solution)/shard_map/all_to_all | solution.py:211
  145.7 0.0 copy-done.2
  145.7 1.5 copy-done.1
  147.2 0.6 finish.1
  147.8 2.2 %collective-permute-start.3 = (bf16[1,225,2048]{2,1,0:T(8,128)(2,1)S(1)}, bf16[1,225,2048]{2,1,0:T(8,128)(2,1)S(1)}, u32[]{:S(2)}, u32[]{:S(2)}) collective-permute-start(bf16[1,225,2048]{2,1,0:T(8,128)(2,1)S(1)} %finish.1), channel_id=1, source_target_pairs={{0,496},{16,0},{32,16},{48,32},{64,48},{80,64},{96,80},{112,96},{1... | collective-permute-start | bytes 2764808 | tf_op jit(solution)/shard_map/ppermute | solution.py:213
  150.0 15.0 %collective-permute-done.3 = bf16[1,225,2048]{2,1,0:T(8,128)(2,1)S(1)} collective-permute-done((bf16[1,225,2048]{2,1,0:T(8,128)(2,1)S(1)}, bf16[1,225,2048]{2,1,0:T(8,128)(2,1)S(1)}, u32[]{:S(2)}, u32[]{:S(2)}) %collective-permute-start.3) | collective-permute-done | bytes 921632 | tf_op jit(solution)/shard_map/ppermute | solution.py:213
  165.0 0.9 copy.11
  (7 shorter events, 0.0 us)
Async XLA Ops:
  0.0 122.9 %copy-start = (f32[64,2048]{1,0:T(8,128)S(1)}, f32[64,2048]{1,0:T(8,128)}, u32[]{:S(2)}) copy-start(f32[64,2048]{1,0:T(8,128)} %param.14) | copy-start | bytes 1572868
  82.5 35.3 %collective-permute-start = (bf16[2,232,2048]{2,1,0:T(8,128)(2,1)}, bf16[2,232,2048]{2,1,0:T(8,128)(2,1)S(1)}, u32[]{:S(2)}, u32[]{:S(2)}) collective-permute-start(bf16[2,232,2048]{2,1,0:T(8,128)(2,1)} %get-tuple-element.18), channel_id=1, source_target_pairs={{16,32},{32,16},{48,64},{64,48},{80,96},{96,80},{112,128},{128,112... | collective-permute-start | bytes 5701640 | tf_op jit(solution)/shard_map/ppermute | solution.py:197
  114.1 8.9 %copy-start.4 = (s32[1,2]{1,0:T(1,128)S(1)}, s32[1,2]{1,0:T(1,128)}, u32[]{:S(2)}) copy-start(s32[1,2]{1,0:T(1,128)} %param.13) | copy-start | bytes 28
  114.1 31.6 %all-to-all-start.1 = ((bf16[16,225,128]{2,1,0:T(8,128)(2,1)}), bf16[16,225,128]{2,1,0:T(8,128)(2,1)S(1)}, u32[]{:S(2)}, u32[]{:S(2)}) async-start(bf16[16,225,128]{2,1,0:T(8,128)(2,1)} %attend.1), calls=%async_computation.1 | async-start | bytes 1900544 | tf_op jit(solution)/shard_map/all_to_all | solution.py:211
  117.9 5.0 %copy-start.5 = (bf16[2,232,2048]{2,1,0:T(8,128)(2,1)}, bf16[2,232,2048]{2,1,0:T(8,128)(2,1)S(1)}, u32[]{:S(2)}) copy-start(bf16[2,232,2048]{2,1,0:T(8,128)(2,1)S(1)} %collective-permute-done.far_ref) | copy-start | bytes 5701636
  117.9 7.5 %collective-permute-start.1 = (bf16[1,225,2048]{2,1,0:T(8,128)(2,1)}, bf16[1,225,2048]{2,1,0:T(8,128)(2,1)}, u32[]{:S(2)}, u32[]{:S(2)}) collective-permute-start(bf16[1,225,2048]{2,1,0:T(8,128)(2,1)} %k_ref.2), channel_id=1, source_target_pairs={{0,16},{16,0},{32,48},{48,32},{64,80},{80,64},{96,112},{112,96},{1... | collective-permute-start | bytes 2764808 | tf_op jit(solution)/shard_map/ppermute | solution.py:208
  119.8 5.6 %collective-permute-start.2 = (bf16[1,225,2048]{2,1,0:T(8,128)(2,1)}, bf16[1,225,2048]{2,1,0:T(8,128)(2,1)}, u32[]{:S(2)}, u32[]{:S(2)}) collective-permute-start(bf16[1,225,2048]{2,1,0:T(8,128)(2,1)} %v_ref.2), channel_id=1, source_target_pairs={{0,16},{16,0},{32,48},{48,32},{64,80},{80,64},{96,112},{112,96},{1... | collective-permute-start | bytes 2764808 | tf_op jit(solution)/shard_map/ppermute | solution.py:209
  125.4 20.2 %copy-start.2 = (bf16[1,225,2048]{2,1,0:T(8,128)(2,1)S(1)}, bf16[1,225,2048]{2,1,0:T(8,128)(2,1)}, u32[]{:S(2)}) copy-start(bf16[1,225,2048]{2,1,0:T(8,128)(2,1)} %residual_ref.1) | copy-start | bytes 2764804
  125.4 20.2 %copy-start.3 = (bf16[225,2048]{1,0:T(8,128)(2,1)S(1)}, bf16[225,2048]{1,0:T(8,128)(2,1)}, u32[]{:S(2)}) copy-start(bf16[225,2048]{1,0:T(8,128)(2,1)} %fresh_ref.1) | copy-start | bytes 2764804
  145.7 1.5 copy-start.1
  147.8 17.2 %collective-permute-start.3 = (bf16[1,225,2048]{2,1,0:T(8,128)(2,1)S(1)}, bf16[1,225,2048]{2,1,0:T(8,128)(2,1)S(1)}, u32[]{:S(2)}, u32[]{:S(2)}) collective-permute-start(bf16[1,225,2048]{2,1,0:T(8,128)(2,1)S(1)} %finish.1), channel_id=1, source_target_pairs={{0,496},{16,0},{32,16},{48,32},{64,48},{80,64},{96,80},{112,96},{1... | collective-permute-start | bytes 2764808 | tf_op jit(solution)/shard_map/ppermute | solution.py:213

commit v5 on v4

--- a/solution.py
+++ b/solution.py
@@ -126,7 +126,7 @@
     )(got)
 
 
-def temporal_kernel(usable_ref, q_ref, k_ref, v_ref, near_k_ref, near_v_ref, far_ref, out_ref):
+def temporal_kernel(usable_ref, q_ref, k_ref, v_ref, near_k_ref, near_v_ref, far_ref, residual_ref, fresh_ref, gate_ref, out_ref):
     rows = q_ref.shape[1]
     for head in range(STEP_HEADS):
         at = columns(head)
@@ -143,10 +143,11 @@
         summed = jnp.zeros_like(q)
         for j in range(3):
             summed += terms[j].astype(jnp.bfloat16).astype(jnp.float32) * values[j].astype(jnp.float32)
-        out_ref[0, :, at] = summed / total
-
-
-def temporal_attend(usable, queries, keys, values, near_keys, near_values, far):
+        base = jnp.where(usable_ref[3] > 0, fresh_ref[:, at].astype(jnp.float32), residual_ref[0, :, at].astype(jnp.float32))
+        out_ref[0, :, at] = base + gate_ref[:, at] * (summed / total)
+
+
+def temporal_attend(usable, queries, keys, values, near_keys, near_values, far, residual, fresh, gate_row):
     _, rows, channels = queries.shape
     width = STEP_HEADS * HEAD_DIM
     spec = pl.BlockSpec((1, rows, width), lambda h: (0, 0, h))
@@ -154,33 +155,32 @@
     return pl.pallas_call(
         temporal_kernel,
         grid=(channels // width,),
-        in_specs=[pl.BlockSpec(memory_space=pltpu.SMEM)] + [spec] * 5 + [pair],
+        in_specs=[pl.BlockSpec(memory_space=pltpu.SMEM)] + [spec] * 5
+        + [pair, spec, pl.BlockSpec((rows, width), lambda h: (0, h)), pl.BlockSpec((1, width), lambda h: (0, h))],
         out_specs=spec,
         out_shape=jax.ShapeDtypeStruct(queries.shape, jnp.float32),
         cost_estimate=pl.CostEstimate(flops=TEMPORAL_FLOPS, bytes_accessed=18 * queries.size, transcendentals=0),
         name="temporal",
-    )(usable, queries, keys, values, near_keys, near_values, far)
-
-
-def finish_kernel(first_ref, spatial_ref, temporal_ref, residual_ref, gate_ref, fresh_ref, out_ref):
-    is_first = first_ref[0] > 0
+    )(usable, queries, keys, values, near_keys, near_values, far, residual, fresh, gate_row)
+
+
+def finish_kernel(spatial_ref, base_ref, gate_ref, out_ref):
     for head in range(spatial_ref.shape[0]):
         at = columns(head)
-        mixed = (spatial_ref[head].astype(jnp.float32) + temporal_ref[0, :, at]).astype(jnp.bfloat16)
-        updated = residual_ref[0, :, at].astype(jnp.float32) + gate_ref[:, at] * mixed.astype(jnp.float32)
-        out_ref[0, :, at] = jnp.where(is_first, fresh_ref[:, at].astype(jnp.float32), updated).astype(jnp.bfloat16)
-
-
-def finish(is_first, spatial, temporal, residual, gate_row, fresh):
+        updated = base_ref[0, :, at] + gate_ref[:, at] * spatial_ref[head].astype(jnp.float32)
+        out_ref[0, :, at] = updated.astype(jnp.bfloat16)
+
+
+def finish(spatial, base, gate_row):
     return pl.pallas_call(
         finish_kernel,
-        in_specs=[pl.BlockSpec(memory_space=pltpu.SMEM)] + [pl.BlockSpec(memory_space=pltpu.VMEM)] * 5,
+        in_specs=[pl.BlockSpec(memory_space=pltpu.VMEM)] * 3,
         out_specs=pl.BlockSpec(memory_space=pltpu.VMEM),
-        out_shape=jax.ShapeDtypeStruct(residual.shape, jnp.bfloat16),
+        out_shape=jax.ShapeDtypeStruct(base.shape, jnp.bfloat16),
         compiler_params=pltpu.CompilerParams(vmem_limit_bytes=16 * MIB),
-        cost_estimate=pl.CostEstimate(flops=4 * residual.size, bytes_accessed=12 * residual.size, transcendentals=0),
+        cost_estimate=pl.CostEstimate(flops=4 * base.size, bytes_accessed=8 * base.size, transcendentals=0),
         name="finish",
-    )(is_first, spatial, temporal, residual, gate_row, fresh)
+    )(spatial, base, gate_row)
 
 
 def on_device(residual, head_queries, head_keys, head_values, levels, window, level_gate, fresh_frame):
@@ -199,17 +199,19 @@
     after = (window[0, 1] >= 1) & (frame <= frames - 2)
     odd = frame % 2 == 1
     near_usable, far_usable = jnp.where(odd, before, after), jnp.where(odd, after, before)
-    usable = jnp.stack([jnp.bool_(True), near_usable, far_usable]).astype(jnp.int32)
-    is_first = (frame == 0).astype(jnp.int32)[None]
-    gate_row = lax.dynamic_slice_in_dim(level_gate, levels[0], 1, axis=0)
+    is_first = frame == 0
+    usable = jnp.stack([jnp.bool_(True), near_usable, far_usable, is_first]).astype(jnp.int32)
+    gate_row = jnp.where(is_first, 0.0, lax.dynamic_slice_in_dim(level_gate, levels[0], 1, axis=0))
     back = attend(got, rows)
     far, head_keys, head_values, _ = lax.optimization_barrier((far, head_keys, head_values, back))
 
     near_keys = lax.ppermute(head_keys, "queue", near_pairs)
     near_values = lax.ppermute(head_values, "queue", near_pairs)
-    temporal = temporal_attend(usable, head_queries, head_keys, head_values, near_keys, near_values, far)
+    base = temporal_attend(
+        usable, head_queries, head_keys, head_values, near_keys, near_values, far, residual, fresh_frame, gate_row
+    )
     spatial = lax.all_to_all(back, "space", split_axis=0, concat_axis=0, tiled=True)
-    updated = finish(is_first, spatial, temporal, residual, gate_row, fresh_frame)
+    updated = finish(spatial, base, gate_row)
     return lax.ppermute(updated, "queue", [(i, (i - 1) % frames) for i in range(frames)])
 
 

time: 166 us -> 166 us (level)
  waiting for transfers between devices: 28.6 us -> 26.6 us
    all_to_all x1, waiting for transfers between devices: 13.6 us -> 11.6 us  [on_device(): lax.all_to_all(back, 'space', split_axis=0, concat_axis=0, tiled=True)]
  transfers between devices with their start and end apart: 5 -> 5, of which waited for: 2 -> 2; matrix products, arithmetic and copies ran while one was open for 1% -> 2% of each run, Pallas kernels for 15% -> 15%
where the time goes in v5:
time: 166 us
  blocking collectives  77.7 us (47%)
  Pallas kernels  30.7 us (18%)
  waiting for transfers between devices  26.6 us (16%)
  starting transfers between devices  23.4 us (14%)
  local copies, waits for them, and re-layouts  3.06 us (2%)
  other arithmetic  2.04 us (1%)
  between operations  2.02 us (1%)
    all_to_all x1, blocking collectives, on_device(): got = lax.all_to_all(sent, 'space', split_axis=0, concat_axis=0, tiled=True)  77.7 us
    pallas_call x1, Pallas kernels, attend(): pl.pallas_call(functools.partial(attend_kernel, sources=sources, main=mai...  18.4 us
    ppermute x1, waiting for transfers between devices, on_device(): lax.ppermute(updated, 'queue', [(i, (i - 1) % frames) for i in range(fram...  15 us
    ppermute x1, starting transfers between devices, on_device(): far = lax.ppermute(own, 'queue', far_pairs)  13.2 us
    all_to_all x1, waiting for transfers between devices, on_device(): lax.all_to_all(back, 'space', split_axis=0, concat_axis=0, tiled=True)  11.6 us
    pallas_call x1, Pallas kernels, temporal_attend(): pl.pallas_call(temporal_kernel, grid=(channels // width,), in_specs=[pl.B...  7.23 us
    pallas_call x1, Pallas kernels, pack(): pl.pallas_call(functools.partial(pack_kernel, main=main), grid=(heads //...  4.79 us
    all_to_all x1, starting transfers between devices, on_device(): lax.all_to_all(back, 'space', split_axis=0, concat_axis=0, tiled=True)  3.77 us
  transfers between devices with their start and end apart: 5, of which 2 were waited for; matrix products, arithmetic and copies ran while one was open for 2% of the time, Pallas kernels for 15%

profile of v5, /device:TPU:7, one launch (start us, length us, event | category | flops | bytes accessed | tf_op | source)
XLA Modules:
  0.0 165.6 jit_solution(14468841020308598833)
XLA Ops:
  0.0 4.8 %pack.1 = (bf16[16,680,128]{2,1,0:T(8,128)(2,1)}, bf16[2,232,2048]{2,1,0:T(8,128)(2,1)}) custom-call(bf16[1,225,2048]{2,1,0:T(8,128)(2,1)} %q_ref.3, bf16[1,225,2048]{2,1,0:T(8,128)(2,1)} %k_ref.2, bf16[1,225,2048]{2,1,0:T(8,128)(2,1)} %v_ref.2), custom_call_target="tpu_custom_call" | custom-call | bytes 7372800 | tf_op jit(solution)/shard_map/pack/pallas_call | solution.py:47
  4.8 77.7 %all_to_all.10.got_ref = bf16[16,680,128]{2,1,0:T(8,128)(2,1)S(1)} all-to-all(bf16[16,680,128]{2,1,0:T(8,128)(2,1)} %get-tuple-element.14), channel_id=1, replica_groups=mesh['queue'=32,'space'=16] {'space'}, dimensions={0} | all-to-all | bytes 5570560 | tf_op jit(solution)/shard_map/all_to_all | solution.py:194
  82.5 13.2 %collective-permute-start = (bf16[2,232,2048]{2,1,0:T(8,128)(2,1)}, bf16[2,232,2048]{2,1,0:T(8,128)(2,1)}, u32[]{:S(2)}, u32[]{:S(2)}) collective-permute-start(bf16[2,232,2048]{2,1,0:T(8,128)(2,1)} %get-tuple-element.18), channel_id=1, source_target_pairs={{16,32},{32,16},{48,64},{64,48},{80,96},{96,80},{112,128},{128,112... | collective-permute-start | bytes 5701640 | tf_op jit(solution)/shard_map/ppermute | solution.py:197
  95.7 18.4 %attend.1 = bf16[16,225,128]{2,1,0:T(8,128)(2,1)} custom-call(bf16[16,680,128]{2,1,0:T(8,128)(2,1)S(1)} %all_to_all.10.got_ref), custom_call_target="tpu_custom_call" | custom-call | flops 6635520000 | bytes 3686400 | tf_op jit(solution)/shard_map/attend/pallas_call | solution.py:110
  114.0 3.8 %all-to-all-start.1 = ((bf16[16,225,128]{2,1,0:T(8,128)(2,1)}), bf16[16,225,128]{2,1,0:T(8,128)(2,1)S(1)}, u32[]{:S(2)}, u32[]{:S(2)}) async-start(bf16[16,225,128]{2,1,0:T(8,128)(2,1)} %attend.1), calls=%async_computation.1 | async-start | bytes 1900544 | tf_op jit(solution)/shard_map/all_to_all | solution.py:213
  117.8 0.0 collective-permute-done.far_ref
  117.8 0.0 copy-done.2
  117.8 1.9 %collective-permute-start.1 = (bf16[1,225,2048]{2,1,0:T(8,128)(2,1)S(1)}, bf16[1,225,2048]{2,1,0:T(8,128)(2,1)}, u32[]{:S(2)}, u32[]{:S(2)}) collective-permute-start(bf16[1,225,2048]{2,1,0:T(8,128)(2,1)S(1)} %copy-done.2), channel_id=1, source_target_pairs={{0,16},{16,0},{32,48},{48,32},{64,80},{80,64},{96,112},{112,96},{1... | collective-permute-start | bytes 2764808 | tf_op jit(solution)/shard_map/ppermute | solution.py:208
  119.8 0.0 copy-done.3
  119.8 2.4 %collective-permute-start.2 = (bf16[1,225,2048]{2,1,0:T(8,128)(2,1)S(1)}, bf16[1,225,2048]{2,1,0:T(8,128)(2,1)}, u32[]{:S(2)}, u32[]{:S(2)}) collective-permute-start(bf16[1,225,2048]{2,1,0:T(8,128)(2,1)S(1)} %copy-done.3), channel_id=1, source_target_pairs={{0,16},{16,0},{32,48},{48,32},{64,80},{80,64},{96,112},{112,96},{1... | collective-permute-start | bytes 2764808 | tf_op jit(solution)/shard_map/ppermute | solution.py:209
  122.9 1.4 broadcast_select_fusion.gate_ref
  124.3 0.0 copy-done.4
  124.3 0.6 fusion
  126.2 0.6 add_convert_fusion.usable_ref
  126.8 0.0 collective-permute-done.1.near_k_ref
  126.8 0.0 collective-permute-done.2.near_v_ref
  126.8 7.2 %temporal.1.base_ref = f32[1,225,2048]{2,1,0:T(8,128)} custom-call(s32[4]{0:T(128)} %add_convert_fusion.usable_ref, bf16[1,225,2048]{2,1,0:T(8,128)(2,1)} %q_ref.3, bf16[1,225,2048]{2,1,0:T(8,128)(2,1)} %k_ref.2, bf16[1,225,2048]{2,1,0:T(8,128)(2,1)} %v_ref.2, bf16[1,225,2048]{2,1,0:T(8,128)(2,1)} %collective-permute-done.1.near_k_ref, ...), custom_call_target="tpu_custom_call" | custom-call | flops 5000000000 | bytes 8294400 | tf_op jit(solution)/shard_map/temporal/pallas_call | solution.py:155
  134.0 11.6 %all-to-all-done.1.spatial_ref = bf16[16,225,128]{2,1,0:T(8,128)(2,1)S(1)} async-done(((bf16[16,225,128]{2,1,0:T(8,128)(2,1)}), bf16[16,225,128]{2,1,0:T(8,128)(2,1)S(1)}, u32[]{:S(2)}, u32[]{:S(2)}) %all-to-all-start.1) | async-done | bytes 921632 | tf_op jit(solution)/shard_map/all_to_all | solution.py:213
  145.6 0.0 copy-done.1
  145.6 1.5 copy-done
  147.1 0.3 finish.1
  147.4 2.2 %collective-permute-start.3 = (bf16[1,225,2048]{2,1,0:T(8,128)(2,1)S(1)}, bf16[1,225,2048]{2,1,0:T(8,128)(2,1)S(1)}, u32[]{:S(2)}, u32[]{:S(2)}) collective-permute-start(bf16[1,225,2048]{2,1,0:T(8,128)(2,1)S(1)} %finish.1), channel_id=1, source_target_pairs={{0,496},{16,0},{32,16},{48,32},{64,48},{80,64},{96,80},{112,96},{1... | collective-permute-start | bytes 2764808 | tf_op jit(solution)/shard_map/ppermute | solution.py:215
  149.6 15.0 %collective-permute-done.3 = bf16[1,225,2048]{2,1,0:T(8,128)(2,1)S(1)} collective-permute-done((bf16[1,225,2048]{2,1,0:T(8,128)(2,1)S(1)}, bf16[1,225,2048]{2,1,0:T(8,128)(2,1)S(1)}, u32[]{:S(2)}, u32[]{:S(2)}) %collective-permute-start.3) | collective-permute-done | bytes 921632 | tf_op jit(solution)/shard_map/ppermute | solution.py:215
  164.6 0.9 copy.11
  (5 shorter events, 0.0 us)
Async XLA Ops:
  82.5 35.4 %collective-permute-start = (bf16[2,232,2048]{2,1,0:T(8,128)(2,1)}, bf16[2,232,2048]{2,1,0:T(8,128)(2,1)}, u32[]{:S(2)}, u32[]{:S(2)}) collective-permute-start(bf16[2,232,2048]{2,1,0:T(8,128)(2,1)} %get-tuple-element.18), channel_id=1, source_target_pairs={{16,32},{32,16},{48,64},{64,48},{80,96},{96,80},{112,128},{128,112... | collective-permute-start | bytes 5701640 | tf_op jit(solution)/shard_map/ppermute | solution.py:197
  114.0 3.8 %copy-start.2 = (bf16[1,225,2048]{2,1,0:T(8,128)(2,1)S(1)}, bf16[1,225,2048]{2,1,0:T(8,128)(2,1)}, u32[]{:S(2)}) copy-start(bf16[1,225,2048]{2,1,0:T(8,128)(2,1)} %k_ref.2) | copy-start | bytes 2764804
  114.0 5.7 %copy-start.3 = (bf16[1,225,2048]{2,1,0:T(8,128)(2,1)S(1)}, bf16[1,225,2048]{2,1,0:T(8,128)(2,1)}, u32[]{:S(2)}) copy-start(bf16[1,225,2048]{2,1,0:T(8,128)(2,1)} %v_ref.2) | copy-start | bytes 2764804
  114.0 10.3 %copy-start.4 = (s32[1,2]{1,0:T(1,128)S(1)}, s32[1,2]{1,0:T(1,128)}, u32[]{:S(2)}) copy-start(s32[1,2]{1,0:T(1,128)} %param.13) | copy-start | bytes 28
  114.0 31.6 %all-to-all-start.1 = ((bf16[16,225,128]{2,1,0:T(8,128)(2,1)}), bf16[16,225,128]{2,1,0:T(8,128)(2,1)S(1)}, u32[]{:S(2)}, u32[]{:S(2)}) async-start(bf16[16,225,128]{2,1,0:T(8,128)(2,1)} %attend.1), calls=%async_computation.1 | async-start | bytes 1900544 | tf_op jit(solution)/shard_map/all_to_all | solution.py:213
  117.8 8.9 %collective-permute-start.1 = (bf16[1,225,2048]{2,1,0:T(8,128)(2,1)S(1)}, bf16[1,225,2048]{2,1,0:T(8,128)(2,1)}, u32[]{:S(2)}, u32[]{:S(2)}) collective-permute-start(bf16[1,225,2048]{2,1,0:T(8,128)(2,1)S(1)} %copy-done.2), channel_id=1, source_target_pairs={{0,16},{16,0},{32,48},{48,32},{64,80},{80,64},{96,112},{112,96},{1... | collective-permute-start | bytes 2764808 | tf_op jit(solution)/shard_map/ppermute | solution.py:208
  119.8 7.0 %collective-permute-start.2 = (bf16[1,225,2048]{2,1,0:T(8,128)(2,1)S(1)}, bf16[1,225,2048]{2,1,0:T(8,128)(2,1)}, u32[]{:S(2)}, u32[]{:S(2)}) collective-permute-start(bf16[1,225,2048]{2,1,0:T(8,128)(2,1)S(1)} %copy-done.3), channel_id=1, source_target_pairs={{0,16},{16,0},{32,48},{48,32},{64,80},{80,64},{96,112},{112,96},{1... | collective-permute-start | bytes 2764808 | tf_op jit(solution)/shard_map/ppermute | solution.py:209
  126.8 18.8 %copy-start.1 = (f32[1,2048]{1,0:T(1,128)S(1)}, f32[1,2048]{1,0:T(1,128)}, u32[]{:S(2)}) copy-start(f32[1,2048]{1,0:T(1,128)} %broadcast_select_fusion.gate_ref) | copy-start | bytes 24580
  145.6 1.5 copy-start
  147.4 17.2 %collective-permute-start.3 = (bf16[1,225,2048]{2,1,0:T(8,128)(2,1)S(1)}, bf16[1,225,2048]{2,1,0:T(8,128)(2,1)S(1)}, u32[]{:S(2)}, u32[]{:S(2)}) collective-permute-start(bf16[1,225,2048]{2,1,0:T(8,128)(2,1)S(1)} %finish.1), channel_id=1, source_target_pairs={{0,496},{16,0},{32,16},{48,32},{64,48},{80,64},{96,80},{112,96},{1... | collective-permute-start | bytes 2764808 | tf_op jit(solution)/shard_map/ppermute | solution.py:215
